TPU v7x, 128 devices: a whole 4x4x4 slice. The times are simulated.
128 devices in a mesh: lon: 32 (over x, y, z_lo), lat: 4 (over z_hi, core).
Axes of the slice: x: 4, y: 4, z: 4 (z_hi: 2, z_lo: 2; z = z_hi * 2 + z_lo), core: 2. Of those that a mesh axis runs over, the one named last changes fastest.
Arguments:
- features: bfloat16 [256, 4096, 512], P('lat', 'lon'), may hold values from -6 to 6
- head_weight: bfloat16 [512, 76], replicated, may hold values from -0.25 to 0.25
- target: bfloat16 [76, 256, 4096], P(None, 'lat', 'lon'), may hold values from -6 to 6
- metrics: float32 [6, 256, 4096], P(None, 'lat', 'lon'), may hold values from 0.5 to 2
- masks: int32 [4, 256, 4096], P(None, 'lat', 'lon'), may hold values 0 or 1
- partner: int32 [4096], replicated, may hold values from 0 to 4095, as said below
Outputs:
- feature_grad: bfloat16 [256, 4096, 512], P('lat', 'lon')
- weight_grad: float32 [512, 76], P('lon')
Inputs may be any that keep to these rules, and one draw needn't show every extreme that they name: partner pairs the columns: partner[partner[i]] = i and partner[i] != i.
All inputs are finite; a program needn't handle non-finite values. No bound on the sum of `masks` on one device may be relied on, other than what follows from the above.
Results may differ from a plain program's by a relative error of at most 0.0049.
Values sent between devices are 32-bit elements; how exact they have to be, the bound alone decides.
A program may use at most 64 MiB of HBM per device.

v0:
```python
import jax
import jax.numpy as jnp
from jax import lax
from jax.sharding import PartitionSpec as P


def padded(block, sides, width, periodic):
    for axis, dim in sides:
        count = lax.axis_size(axis)
        forward = [(i, i + 1) for i in range(count - 1)]
        if periodic:
            forward.append((count - 1, 0))
        backward = [(target, source) for source, target in forward]
        low = lax.ppermute(
            lax.slice_in_dim(block, block.shape[dim] - width, None, axis=dim), axis, forward
        )
        high = lax.ppermute(lax.slice_in_dim(block, 0, width, axis=dim), axis, backward)
        block = jnp.concatenate([low, block, high], axis=dim)
    return block


def zonal_edges(first, second):
    widened = padded(jnp.concatenate([first, second], 0), (("lon", 2),), 1, True)
    split_at = first.shape[0]
    return (widened[:split_at, :, 2:], widened[split_at:, :, :-2])


def meridional_edges(first, second):
    widened = padded(jnp.concatenate([first, second], 0), (("lat", 1),), 1, False)
    split_at = first.shape[0]
    return (widened[:split_at, 2:, :], widened[split_at:, :-2, :])


def fold_row(top_row):
    return lax.all_gather(top_row, "lon", axis=1, tiled=True)


def replace_top(field, new_row):
    return jnp.concatenate([field[:, :-1, :], new_row[:, None, :]], 1)


def per_device(features, head_weight, target, metrics, masks, partner):
    lat_rows, lon_cells, feat_width = features.shape
    levels = target.shape[0] // 4
    cell_rows = features.reshape(lat_rows * lon_cells, feat_width)
    contract = (((0,), (1,)), ((), ()))
    predicted = lax.dot_general(
        head_weight, cell_rows, contract, preferred_element_type=jnp.float32
    )
    errors = predicted.reshape(4 * levels, lat_rows, lon_cells) - target.astype(jnp.float32)
    weights = masks.astype(jnp.float32)
    top_band = lax.axis_index("lat") == lax.axis_size("lat") - 1
    col_start = lax.axis_index("lon") * lon_cells
    mirror = lax.dynamic_slice_in_dim(partner, col_start, lon_cells, 0)
    u_err = errors[:levels] * weights[0]
    v_err = errors[levels : 2 * levels] * weights[1]
    other = errors[2 * levels :] * weights[3]
    u_flux = metrics[0] * u_err
    v_flux = metrics[3] * v_err
    u_across = metrics[1] * u_err
    v_across = metrics[2] * v_err
    corner_weight = weights[2] / metrics[4]
    centre_weight = weights[3] / metrics[5]
    v_east, uy_west = zonal_edges(v_flux, u_across)
    u_north, vx_south = meridional_edges(u_flux, v_across)
    top_flux = u_flux[:, -1, :]
    mirror_flux = jnp.take(fold_row(top_flux), mirror, axis=1)
    u_north = replace_top(u_north, jnp.where(top_band, -mirror_flux, u_north[:, -1, :]))
    vorticity = corner_weight * (v_east - v_flux - u_north + u_flux)
    shear = corner_weight * (u_north - u_flux + v_east - v_flux)
    tension = centre_weight * (u_across - uy_west - v_across + vx_south)
    co_vort = weights[2] * vorticity
    co_shear = weights[2] * shear
    co_tension = weights[3] * tension
    summed = co_vort + co_shear
    differ = co_vort - co_shear
    tension_east, summed_west = zonal_edges(co_tension, summed)
    tension_north, differ_south = meridional_edges(co_tension, differ)
    grad_v = summed_west - summed
    grad_u = differ - differ_south
    fold_term = jnp.take(fold_row(differ[:, -1, :]), mirror, axis=1)
    grad_u = replace_top(grad_u, grad_u[:, -1, :] + jnp.where(top_band, fold_term, 0.0))
    grad_uy = co_tension - tension_east
    grad_vx = tension_north - co_tension
    grad_ue = weights[0] * (metrics[0] * grad_u + metrics[1] * grad_uy)
    grad_ve = weights[1] * (metrics[3] * grad_v + metrics[2] * grad_vx)
    grad_other = metrics[5] * other
    grads = jnp.concatenate([grad_ue, grad_ve, grad_other], 0)
    grads = grads.reshape(4 * levels, lat_rows * lon_cells).astype(jnp.bfloat16)
    feature_grad = lax.dot_general(grads, head_weight, contract, preferred_element_type=jnp.float32)
    feature_grad = feature_grad.astype(jnp.bfloat16).reshape(lat_rows, lon_cells, feat_width)
    total_cells = lat_rows * lax.axis_size("lat") * lon_cells * lax.axis_size("lon")
    lon_rows = lax.psum_scatter(
        lax.dot_general(cell_rows, grads, contract, preferred_element_type=jnp.float32)
        / total_cells,
        "lon",
        scatter_dimension=0,
        tiled=True,
    )
    weight_grad = lax.psum(lon_rows, "lat")
    return (feature_grad, weight_grad)


def solution(mesh):
    return jax.shard_map(
        per_device,
        mesh=mesh,
        in_specs=(
            P("lat", "lon", None),
            P(),
            P(None, "lat", "lon"),
            P(None, "lat", "lon"),
            P(None, "lat", "lon"),
            P(),
        ),
        out_specs=(P("lat", "lon", None), P("lon", None)),
        check_vma=False,
    )
```

profile of v0, /device:TPU:1, one launch (start us, length us, event | category | flops | bytes accessed | tf_op | source)
XLA Modules:
  0.0 422.0 jit_solution(7365571106989394282)
XLA Ops:
  7.2 0.9 convert_element_type.16
  9.0 6.3 %convert_subtract_fusion = f32[76,64,128]{2,0,1:T(8,128)S(1)} fusion(bf16[64,128,512]{2,1,0:T(8,128)(2,1)} %param.8, bf16[76,64,128]{2,1,0:T(8,128)(2,1)} %param.10, bf16[512,76]{0,1:T(8,128)(2,1)S(1)} %copy-done), kind=kOutput, calls=%fused_computation.4 | convolution fusion | flops 638779392 | bytes 12201984 | tf_op jit(solution)/shard_map/dot_general | solution.py:47
  15.7 1.1 copy-done.3
  16.9 3.3 collective-permute-start.1
  20.2 5.5 %collective-permute-start.3 = (f32[38,1,128]{2,0,1:T(8,128)S(1)}, f32[38,1,128]{2,0,1:T(8,128)S(1)}, u32[]{:S(2)}, u32[]{:S(2)}) collective-permute-start(f32[38,1,128]{2,0,1:T(8,128)S(1)} %get-tuple-element.28), channel_id=1, source_target_pairs={{0,1},{1,2},{2,3},{4,5},{5,6},{6,7},{8,9},{9,10},{10,11},{12,13},{... | collective-permute-start | bytes 58376 | tf_op jit(solution)/shard_map/ppermute | solution.py:14
  25.7 2.0 slice_maximum_fusion
  27.7 1.7 copy.26
  30.2 1.7 copy.22
  32.0 5.0 %collective-permute-start = (f32[38,64,1]{1,2,0:T(1,128)S(1)}, f32[38,64,1]{1,2,0:T(1,128)S(1)}, u32[]{:S(2)}, u32[]{:S(2)}) collective-permute-start(f32[38,64,1]{1,2,0:T(1,128)S(1)} %copy.22), channel_id=1, source_target_pairs={{4,0},{8,4},{12,8},{16,12},{20,16},{24,20},{28,24},{32,28},{36,32}... | collective-permute-start | bytes 29192 | tf_op jit(solution)/shard_map/ppermute | solution.py:17
  37.0 64.7 %all-gather = f32[19,1,4096]{2,0,1:T(8,128)S(1)} all-gather(f32[19,1,128]{2,0,1:T(8,128)S(1)} %slice.173), channel_id=2, replica_groups=mesh['lon'=32,'lat'=4] {'lon'}, dimensions={2}, use_global_device_ids=true | all-gather | bytes 321024 | tf_op jit(solution)/shard_map/all_gather | solution.py:35
  102.4 2.5 fusion.1
  104.9 0.9 slice.172
  105.9 2.0 copy.24
  107.8 2.2 gather_fusion
  110.1 1.6 copy.23
  111.7 1.6 copy.27
  113.9 3.2 fusion.30
  118.0 17.6 %collective-permute-start.4 = (f32[38,1,128]{2,0,1:T(8,128)}, f32[38,1,128]{2,0,1:T(8,128)}, u32[]{:S(2)}, u32[]{:S(2)}) collective-permute-start(f32[38,1,128]{2,0,1:T(8,128)} %get-tuple-element.23), channel_id=1, source_target_pairs={{0,1},{1,2},{2,3},{4,5},{5,6},{6,7},{8,9},{9,10},{10,11},{12,13},{... | collective-permute-start | bytes 58376 | tf_op jit(solution)/shard_map/ppermute | solution.py:14
  135.6 1.9 collective-permute-start.7
  137.6 1.6 fusion
  139.2 2.4 copy.30
  141.5 1.1 copy.32
  142.6 5.7 %collective-permute-start.5 = (f32[38,64,1]{1,2,0:T(1,128)}, f32[38,64,1]{1,2,0:T(1,128)}, u32[]{:S(2)}, u32[]{:S(2)}) collective-permute-start(f32[38,64,1]{1,2,0:T(1,128)} %copy.30), channel_id=1, source_target_pairs={{4,0},{8,4},{12,8},{16,12},{20,16},{24,20},{28,24},{32,28},{36,32}... | collective-permute-start | bytes 29192 | tf_op jit(solution)/shard_map/ppermute | solution.py:17
  148.3 63.6 %all-gather.1 = f32[19,1,4096]{2,0,1:T(8,128)S(1)} all-gather(f32[19,1,128]{2,0,1:T(8,128)S(1)} %slice-done), channel_id=3, replica_groups=mesh['lon'=32,'lat'=4] {'lon'}, dimensions={2}, use_global_device_ids=true | all-gather | bytes 321024 | tf_op jit(solution)/shard_map/all_gather | solution.py:35
  213.4 1.3 copy.31
  214.7 2.3 copy.33
  219.1 1.7 fusion.13
  221.4 4.9 %fusion.3 = f32[512,76]{0,1:T(8,128)S(1)} fusion(bf16[76,64,128]{2,0,1:T(8,128)(2,1)S(1)} %maximum_convert_fusion, bf16[64,128,512]{2,1,0:T(8,128)(2,1)} %param.8), kind=kOutput, calls=%fused_computation.16 | convolution fusion | flops 637573120 | bytes 9789440 | tf_op jit(solution)/shard_map/dot_general | solution.py:94
  226.8 1.0 copy.38
  228.6 5.8 %convolution_convert_fusion = bf16[8192,512]{1,0:T(8,128)(2,1)} fusion(bf16[76,8192]{1,0:T(8,128)(2,1)S(1)} %bitcast.70, bf16[512,76]{0,1:T(8,128)(2,1)S(1)} %copy-done), kind=kOutput, calls=%fused_computation.2 | convolution fusion | flops 641728512 | bytes 9711616 | tf_op jit(solution)/shard_map/dot_general | solution.py:90
  234.4 139.9 %reduce-scatter.4.cloned.1.call-done = f32[16,76]{1,0:T(8,128)} async-done(((f32[512,76]{1,0:T(8,128)}), f32[16,76]{1,0:T(8,128)}) %reduce-scatter.4.cloned.1.call-update) | async-done | bytes 4880
  375.0 39.4 %psum.7 = f32[16,76]{0,1:T(8,128)S(1)} all-reduce(f32[16,76]{0,1:T(8,128)S(1)} %copy.37), channel_id=1, replica_groups=mesh['lon'=32,'lat'=4] {'lat'}, use_global_device_ids=true, to_apply=%region_1.3 | all-reduce | flops 1216 | bytes 9728 | tf_op jit(solution)/shard_map/psum | solution.py:100
  (61 shorter events, 11.3 us)
Async XLA Ops:
  7.2 1.9 copy-start
  7.2 367.1 %reduce-scatter.4.cloned.1.call-start = ((), (), s32[]{:S(2)}) async-start(), calls=%async_computation.1 | async-start | bytes 270336
  15.4 1.5 copy-start.3
  16.9 10.8 %copy-start.4 = (f32[19,64,128]{2,0,1:T(8,128)}, f32[19,64,128]{2,0,1:T(8,128)S(1)}, u32[]{:S(2)}) copy-start(f32[19,64,128]{2,0,1:T(8,128)S(1)} %get-tuple-element.19) | copy-start | bytes 1867780
  16.9 96.4 %collective-permute-start.1 = (f32[38,1,128]{2,0,1:T(8,128)S(1)}, f32[38,1,128]{2,0,1:T(8,128)S(1)}, u32[]{:S(2)}, u32[]{:S(2)}) collective-permute-start(f32[38,1,128]{2,0,1:T(8,128)S(1)} %get-tuple-element.27), channel_id=1, source_target_pairs={{1,0},{2,1},{3,2},{5,4},{6,5},{7,6},{9,8},{10,9},{11,10},{13,12},{... | collective-permute-start | bytes 58376 | tf_op jit(solution)/shard_map/ppermute | solution.py:17
  20.2 93.1 %collective-permute-start.3 = (f32[38,1,128]{2,0,1:T(8,128)S(1)}, f32[38,1,128]{2,0,1:T(8,128)S(1)}, u32[]{:S(2)}, u32[]{:S(2)}) collective-permute-start(f32[38,1,128]{2,0,1:T(8,128)S(1)} %get-tuple-element.28), channel_id=1, source_target_pairs={{0,1},{1,2},{2,3},{4,5},{5,6},{6,7},{8,9},{9,10},{10,11},{12,13},{... | collective-permute-start | bytes 58376 | tf_op jit(solution)/shard_map/ppermute | solution.py:14
  29.4 82.3 %collective-permute-start.2 = (f32[38,64,1]{1,2,0:T(1,128)S(1)}, f32[38,64,1]{1,2,0:T(1,128)S(1)}, u32[]{:S(2)}, u32[]{:S(2)}) collective-permute-start(f32[38,64,1]{1,2,0:T(1,128)S(1)} %copy.26), channel_id=1, source_target_pairs={{0,4},{4,8},{8,12},{12,16},{16,20},{20,24},{24,28},{28,32},{32,36}... | collective-permute-start | bytes 29192 | tf_op jit(solution)/shard_map/ppermute | solution.py:14
  32.0 78.2 %collective-permute-start = (f32[38,64,1]{1,2,0:T(1,128)S(1)}, f32[38,64,1]{1,2,0:T(1,128)S(1)}, u32[]{:S(2)}, u32[]{:S(2)}) collective-permute-start(f32[38,64,1]{1,2,0:T(1,128)S(1)} %copy.22), channel_id=1, source_target_pairs={{4,0},{8,4},{12,8},{16,12},{20,16},{24,20},{28,24},{32,28},{36,32}... | collective-permute-start | bytes 29192 | tf_op jit(solution)/shard_map/ppermute | solution.py:17
  102.4 10.9 %copy-start.11 = (pred[128]{0:T(512)(128)(4,1)}, pred[128]{0:T(512)(128)(4,1)S(1)}, u32[]{:S(2)}) copy-start(pred[128]{0:T(512)(128)(4,1)S(1)} %get-tuple-element.12) | copy-start | bytes 388
  104.9 2.9 copy-start.10
  113.3 0.6 copy-start.9
  117.1 20.5 %copy-start.5 = (f32[19,64,128]{2,0,1:T(8,128)}, f32[19,64,128]{2,0,1:T(8,128)S(1)}, u32[]{:S(2)}) copy-start(f32[19,64,128]{2,0,1:T(8,128)S(1)} %get-tuple-element.9) | copy-start | bytes 1867780
  117.2 22.0 %copy-start.1 = (f32[19,64,128]{2,0,1:T(8,128)}, f32[19,64,128]{2,0,1:T(8,128)S(1)}, u32[]{:S(2)}) copy-start(f32[19,64,128]{2,0,1:T(8,128)S(1)} %sub.41) | copy-start | bytes 1867780
  118.0 99.0 %collective-permute-start.4 = (f32[38,1,128]{2,0,1:T(8,128)}, f32[38,1,128]{2,0,1:T(8,128)}, u32[]{:S(2)}, u32[]{:S(2)}) collective-permute-start(f32[38,1,128]{2,0,1:T(8,128)} %get-tuple-element.23), channel_id=1, source_target_pairs={{0,1},{1,2},{2,3},{4,5},{5,6},{6,7},{8,9},{9,10},{10,11},{12,13},{... | collective-permute-start | bytes 58376 | tf_op jit(solution)/shard_map/ppermute | solution.py:14
  135.6 82.3 %collective-permute-start.7 = (f32[38,1,128]{2,0,1:T(8,128)}, f32[38,1,128]{2,0,1:T(8,128)}, u32[]{:S(2)}, u32[]{:S(2)}) collective-permute-start(f32[38,1,128]{2,0,1:T(8,128)} %get-tuple-element.24), channel_id=1, source_target_pairs={{1,0},{2,1},{3,2},{5,4},{6,5},{7,6},{9,8},{10,9},{11,10},{13,12},{... | collective-permute-start | bytes 58376 | tf_op jit(solution)/shard_map/ppermute | solution.py:17
  139.2 9.1 %slice-start = ((f32[19,64,128]{2,0,1:T(8,128)}), f32[19,1,128]{2,0,1:T(8,128)S(1)}, s32[]{:S(2)}) async-start(f32[19,64,128]{2,0,1:T(8,128)} %copy-done.1), calls=%async_computation.2 | async-start | bytes 24576 | tf_op jit(solution)/shard_map/slice | solution.py:81
  142.6 72.1 %collective-permute-start.6 = (f32[38,64,1]{1,2,0:T(1,128)}, f32[38,64,1]{1,2,0:T(1,128)}, u32[]{:S(2)}, u32[]{:S(2)}) collective-permute-start(f32[38,64,1]{1,2,0:T(1,128)} %copy.32), channel_id=1, source_target_pairs={{0,4},{4,8},{8,12},{12,16},{16,20},{20,24},{24,28},{28,32},{32,36}... | collective-permute-start | bytes 29192 | tf_op jit(solution)/shard_map/ppermute | solution.py:14
  142.6 70.8 %collective-permute-start.5 = (f32[38,64,1]{1,2,0:T(1,128)}, f32[38,64,1]{1,2,0:T(1,128)}, u32[]{:S(2)}, u32[]{:S(2)}) collective-permute-start(f32[38,64,1]{1,2,0:T(1,128)} %copy.30), channel_id=1, source_target_pairs={{4,0},{8,4},{12,8},{16,12},{20,16},{24,20},{28,24},{32,28},{36,32}... | collective-permute-start | bytes 29192 | tf_op jit(solution)/shard_map/ppermute | solution.py:17
  213.3 3.6 copy-start.2
  216.9 0.9 copy-start.12
  217.0 1.3 copy-start.7
  217.9 1.2 copy-start.6
  218.0 2.9 copy-start.8
Sparse Core Ops, SparseCore 0:
  228.7 145.4 reduce-scatter.3
where the time goes:
time: 423 us; the launch traced here: 422 us
  blocking collectives  168 us (40%)
  waiting for transfers between devices  140 us (33%)
  starting transfers between devices  39.9 us (9%)
  local copies, waits for them, and re-layouts  26.9 us (6%)
  matrix products  17 us (4%)
  other arithmetic  16.3 us (4%)
  between operations  14.3 us (3%)
    unnamed x2, waiting for transfers between devices  140 us
    all_gather x2, blocking collectives, fold_row(): return lax.all_gather(top_row, 'lon', axis=1, tiled=True)  128 us
    psum x1, blocking collectives, per_device(): weight_grad = lax.psum(lon_rows, 'lat')  39.4 us
    ppermute x4, starting transfers between devices, padded(): lax.ppermute(lax.slice_in_dim(block, block.shape[dim] - width, None, axis...  23.9 us
    ppermute x4, starting transfers between devices, padded(): lax.ppermute(lax.slice_in_dim(block, 0, width, axis=dim), axis, backward)  15.9 us
  transfers between devices with their start and end apart: 9, of which 1 were waited for; matrix products, arithmetic and copies ran while one was open for 8% of the time, Pallas kernels for 0%

commit v1 on v0

v1 whole, which is shorter than its diff:
```python
import functools

import jax
import jax.numpy as jnp
from jax import lax
from jax.experimental import pallas as pl
from jax.experimental.pallas import tpu as pltpu
from jax.sharding import PartitionSpec as P

LEV = 19
CHP = 96
ROW = 56
MESH = pl.DeviceIdType.MESH
F32 = jnp.float32
BF16 = jnp.bfloat16
NT = (((1,), (1,)), ((), ()))


def lanes(shape):
    return lax.broadcasted_iota(jnp.int32, shape, len(shape) - 1)


def grads_kernel(
    feat, tgt, met, msk, wt, part, gr_out, wp_out, wg_out,
    F, Tb, Tf, M, K, Wv, Pv, Wp, EG, ED, HW, HE, CNW, CSE, CW, FS, FB, GR, ACC, WS, RB, LB,
    fsem, lsem, gsem, hs, hr, fs_s, fs_r, rs_s, rs_r, ls_s, ls_r,
):
    n_lon, n_lat = lax.axis_size("lon"), lax.axis_size("lat")
    lon, lat = lax.axis_index("lon"), lax.axis_index("lat")
    R = tgt.shape[1]
    C = tgt.shape[2]
    ft = feat.shape[1]
    n16 = R // 16
    n8 = R // 8
    cells16 = 16 * C
    cells8 = 8 * C
    blk = ft // n_lon
    top = lat == n_lat - 1
    bottom = lat == 0
    east = lax.rem(lon + 1, n_lon)
    west = lax.rem(lon + n_lon - 1, n_lon)
    up = lax.rem(lat + 1, n_lat)
    down = lax.rem(lat + n_lat - 1, n_lat)

    def fcopy(c):
        at = pl.ds(pl.multiple_of(c * cells16, cells16), cells16)
        return pltpu.make_async_copy(feat.at[at], F.at[at], fsem.at[c])

    small = [
        pltpu.make_async_copy(met, M, lsem.at[0]),
        pltpu.make_async_copy(msk, K, lsem.at[1]),
        pltpu.make_async_copy(wt, Wv, lsem.at[2]),
        pltpu.make_async_copy(part, Pv, lsem.at[3]),
        pltpu.make_async_copy(tgt, Tb, lsem.at[4]),
    ]
    for copy in small:
        copy.start()
    for i in range(n16):
        fcopy((i + n16 - 1) % n16).start()

    @pl.when(bottom)
    def _():
        EG[0:ROW, :] = jnp.zeros((ROW, C), F32)
        CSE[...] = jnp.zeros_like(CSE)

    @pl.when(top)
    def _():
        EG[(R + 1) * ROW : (R + 2) * ROW, :] = jnp.zeros((ROW, C), F32)
        CNW[...] = jnp.zeros_like(CNW)

    barrier = pltpu.get_barrier_semaphore()

    @pl.loop(1, n_lon)
    def _(d):
        pl.semaphore_signal(
            barrier, inc=1, device_id=(lax.rem(lon + d, n_lon), lat), device_id_type=MESH
        )

    for d in range(1, n_lat):
        pl.semaphore_signal(
            barrier, inc=1, device_id=(lon, lax.rem(lat + d, n_lat)), device_id_type=MESH
        )
    pl.semaphore_signal(barrier, inc=1, device_id=(east, down), device_id_type=MESH)
    pl.semaphore_signal(barrier, inc=1, device_id=(west, up), device_id_type=MESH)

    small[0].wait()
    small[1].wait()
    for g in range(n8):
        at = slice(8 * g, 8 * g + 8)
        um, vm = K[0, at, :].astype(F32), K[1, at, :].astype(F32)
        qm, hm = K[2, at, :].astype(F32), K[3, at, :].astype(F32)
        area_h = M[5, at, :]
        qw = 2.0 * qm / M[4, at, :]
        coefs = (
            M[0, at, :] * um, M[1, at, :] * um, M[3, at, :] * vm, M[2, at, :] * vm,
            qw, hm / area_h, area_h * hm, qw,
        )
        for k, value in enumerate(coefs):
            EG[pl.ds((8 * g + 1) * ROW + 24 + k, 8, stride=ROW), :] = value

    small[2].wait()
    p = lax.broadcasted_iota(jnp.int32, (CHP, 4 * LEV), 0)
    c = lax.broadcasted_iota(jnp.int32, (CHP, 4 * LEV), 1)
    pick = ((p < 19) & (c == p)) | ((p >= 24) & (p < 43) & (c == p - 5))
    pick = pick | ((p >= 48) & (p < 86) & (c == p - 10))
    wp = lax.dot_general(
        jnp.where(pick, 1.0, 0.0).astype(BF16), Wv[...], NT, preferred_element_type=F32
    )
    Wp[...] = wp.astype(BF16)
    wp_copy = pltpu.make_async_copy(Wp, wp_out, lsem.at[5])
    wp_copy.start()
    ED[...] = jnp.zeros_like(ED)
    Tf[4 * LEV * R :, :] = jnp.zeros((4 * R, C), F32)
    small[3].wait()
    small[4].wait()

    def send(src, dst, k, device):
        return pltpu.make_async_remote_copy(
            src_ref=src, dst_ref=dst, send_sem=hs.at[k], recv_sem=hr.at[k],
            device_id=device, device_id_type=MESH,
        )

    south_row = EG.at[0:ROW]
    first_row = EG.at[ROW : 2 * ROW]
    last_row = EG.at[R * ROW : (R + 1) * ROW]
    north_row = EG.at[(R + 1) * ROW : (R + 2) * ROW]
    to_north = send(last_row, south_row, 0, (lon, up))
    to_south = send(first_row, north_row, 1, (lon, down))
    to_east = send(ED, HW, 2, (east, lat))
    to_west = send(ED, HE, 3, (west, lat))
    to_nw = send(EG.at[R * ROW + 24 : (R + 1) * ROW], CSE, 4, (west, up))
    to_se = send(EG.at[ROW : ROW + 32], CNW, 5, (east, down))

    def fold_copy(peer, d, slot):
        return pltpu.make_async_remote_copy(
            src_ref=FS, dst_ref=FB.at[slot], send_sem=fs_s.at[d], recv_sem=fs_r.at[slot],
            device_id=(peer, lat), device_id_type=MESH,
        )

    def errors_chunk(i, _):
        chunk = lax.rem(i + n16 - 1, n16)
        r0 = pl.multiple_of(chunk * 16, 16)
        fcopy(chunk).wait()
        for ch in range(4 * LEV):
            at = pl.ds(pl.multiple_of(ch * R + r0, 16), 16)
            Tf[at, :] = Tb[ch, pl.ds(r0, 16), :].astype(F32)
        half = lanes((ROW, C)) >> 1
        packed = ED[...]
        for j4 in range(4):
            cells = pl.ds(pl.multiple_of(chunk * cells16 + j4 * 4 * C, 4 * C), 4 * C)
            predicted = lax.dot_general(Wp[...], F[cells, :], NT, preferred_element_type=F32)
            for j in range(4):
                r = r0 + 4 * j4 + j
                base = pl.multiple_of((r + 1) * ROW, 8)
                mine = predicted[:, j * C : (j + 1) * C]

                def true_at(first, count):
                    return jnp.concatenate(
                        [Tf[pl.ds((first + 8 * k) * R + r, 8, stride=R), :] for k in range(count)], 0
                    )

                EG[pl.ds(base, 24), :] = mine[0:24] - true_at(0, 3)
                EG[pl.ds(base + 32, 24), :] = mine[24:48] - true_at(LEV, 3)
                other = (mine[48:88] - true_at(2 * LEV, 5)) * EG[pl.ds(base + 30, 1), :]
                other = jnp.concatenate([other, jnp.zeros((8, C), F32)], 0)
                q = 4 * j4 + j
                GR[2 * chunk + q // 8, 48:CHP, (q % 8) * C : (q % 8 + 1) * C] = other.astype(BF16)
                packed = jnp.where(
                    half == r, pltpu.roll(EG[pl.ds(base, ROW), :], 2 * r + 1, 1), packed
                )
        ED[...] = packed

        @pl.when(i == 0)
        def _():
            pl.semaphore_wait(barrier, n_lon + n_lat)

            @pl.when(jnp.logical_not(top))
            def _():
                to_north.start()
                to_nw.start()

            @pl.when(top)
            def _():
                row = R * ROW
                flux = EG[row : row + 24, :] * EG[row + 24 : row + 25, :]
                sub = lax.broadcasted_iota(jnp.int32, (24, C), 0)
                FS[...] = jnp.where(sub == 23, EG[row + 28 : row + 29, :], flux)

                @pl.loop(1, n_lon)
                def _(d):
                    fold_copy(lax.rem(lon + d, n_lon), d, lon).start()

                FB[lon] = FS[...]

        @pl.when(i == 1)
        def _():
            @pl.when(jnp.logical_not(bottom))
            def _():
                to_south.start()
                to_se.start()

        return 0

    lax.fori_loop(0, n16, errors_chunk, 0)
    to_east.start()
    to_west.start()

    @pl.when(jnp.logical_not(bottom))
    def _():
        to_north.wait_recv()
        to_nw.wait_recv()

    to_east.wait_recv()
    to_west.wait_recv()

    wide = (24, C)
    lane = lanes(wide)
    even = (lane & 1) == 0

    def roll(x, by):
        return pltpu.roll(x, by, 1)

    he = roll(HE[...], C - 1)
    hw = roll(HW[...], 1)
    ed = ED[...]
    flux_e = he[32:56] * he[26:27]
    across_e = he[32:56] * he[27:28]
    corner = CSE[8:32, :] * CSE[3:4, :]
    before = jnp.where(lane == 0, corner, roll(across_e, 2))
    tension_e = he[29:30] * (he[0:24] * he[25:26] - ed[0:24] * ed[25:26] - across_e + before)
    across_w = hw[0:24] * hw[25:26]
    summed_w = hw[28:29] * (ed[32:56] * ed[26:27] - hw[32:56] * hw[26:27])
    edge_a = jnp.where(even, flux_e, across_w)
    edge_b = jnp.where(even, tension_e, summed_w)

    def u_at(base):
        return EG[pl.ds(base, 24), :]

    def v_at(base):
        return EG[pl.ds(base + 32, 24), :]

    def coef(base, k):
        return EG[pl.ds(base + 24 + k, 1), :]

    def shifted_west(x, edge):
        return jnp.where(lane == 0, edge, roll(x, 1))

    def shifted_east(x, edge):
        return jnp.where(lane == C - 1, edge, roll(x, C - 1))

    uf0 = u_at(ROW) * coef(ROW, 0)
    va0 = v_at(ROW) * coef(ROW, 3)
    ra0 = roll(edge_a, C - 1)
    ua0 = u_at(ROW) * coef(ROW, 1)
    ct0 = coef(ROW, 5) * (ua0 - shifted_west(ua0, ra0) - va0 + v_at(0) * coef(0, 3))
    df0 = coef(0, 7) * (u_at(0) * coef(0, 0) - uf0)

    ACC[...] = jnp.zeros_like(ACC)
    CW[...] = jnp.zeros_like(CW)

    def stencil_chunk(i, carry):
        uf, va, ct, df, ra = carry
        last = i == n8 - 1

        @pl.when(last)
        def _():
            @pl.when(jnp.logical_not(top))
            def _():
                to_south.wait_recv()
                to_se.wait_recv()

            CW[...] = roll(CNW[0:24, :] * CNW[25:26, :], 1)

            @pl.when(top)
            def _():
                @pl.loop(1, n_lon)
                def _(d):
                    slot = lax.rem(lon + n_lon - d, n_lon)
                    fold_copy(slot, d, slot).wait_recv()

                mirror = Pv[pl.ds(lon, 1), :]
                which = jnp.broadcast_to(mirror >> 7, wide)
                within = jnp.broadcast_to(mirror & 127, wide)

                def look(b, found):
                    there = jnp.take_along_axis(FB[b], within, axis=1, mode="promise_in_bounds")
                    return jnp.where(which == b, there, found)

                found = lax.fori_loop(0, n_lon, look, jnp.zeros(wide, F32))
                beyond = (R + 1) * ROW
                EG[beyond : beyond + 24, :] = -found
                EG[beyond + 24 : beyond + 25, :] = jnp.ones((1, C), F32)
                at = R * ROW + 31
                EG[at : at + 1, :] = EG[at : at + 1, :] + found[23:24]

        for j in range(8):
            r = 8 * i + j
            b0 = pl.multiple_of((r + 1) * ROW, 8)
            b1 = pl.multiple_of((r + 2) * ROW, 8)
            u1, v1 = u_at(b1), v_at(b1)
            uf1, ua1, va1 = u1 * coef(b1, 0), u1 * coef(b1, 1), v1 * coef(b1, 3)
            ra1 = roll(edge_a, lax.rem(4 * C - 3 - 2 * r, C))
            if j == 7:
                ra1 = jnp.where(last, CW[...], ra1)
            rb = roll(edge_b, C - 1 - 2 * r)
            df1 = coef(b0, 7) * (uf - uf1)
            ct1 = coef(b1, 5) * (ua1 - shifted_west(ua1, ra1) - va1 + va)
            vf = v_at(b0) * coef(b0, 2)
            summed = coef(b0, 4) * (shifted_east(vf, ra) - vf)
            grad_v = shifted_west(summed, rb) - summed
            grad_uy = ct - shifted_east(ct, rb)
            gu = coef(b0, 0) * (df1 - df) + coef(b0, 1) * grad_uy
            gv = coef(b0, 2) * grad_v + coef(b0, 3) * (ct1 - ct)
            GR[i, 0:48, j * C : (j + 1) * C] = jnp.concatenate([gu, gv], 0).astype(BF16)
            uf, va, ct, df, ra = uf1, va1, ct1, df1, ra1
        pltpu.make_async_copy(GR.at[i], gr_out.at[i], gsem.at[i]).start()
        cells = pl.ds(pl.multiple_of(i * cells8, cells8), cells8)
        ACC[...] += jnp.dot(GR[i], F[cells, :], preferred_element_type=F32)
        return uf, va, ct, df, ra

    lax.fori_loop(0, n8, stencil_chunk, (uf0, va0, ct0, df0, ra0))

    scale = 1.0 / (R * n_lat * C * n_lon)
    acc = ACC[...] * scale
    acc = jnp.concatenate([acc, jnp.zeros((C - CHP, ft), F32)], 0)
    WS[...] = acc.T

    def rows_copy(peer, d, slot):
        src = WS.at[pl.ds(pl.multiple_of(peer * blk, blk), blk)]
        return pltpu.make_async_remote_copy(
            src_ref=src, dst_ref=RB.at[slot], send_sem=rs_s.at[d], recv_sem=rs_r.at[slot],
            device_id=(peer, lat), device_id_type=MESH,
        )

    @pl.loop(1, n_lon)
    def _(d):
        rows_copy(lax.rem(lon + d, n_lon), d, lon).start()

    RB[lon] = WS[pl.ds(pl.multiple_of(lon * blk, blk), blk), :]

    @pl.loop(1, n_lon)
    def _(d):
        slot = lax.rem(lon + n_lon - d, n_lon)
        rows_copy(slot, d, slot).wait_recv()

    total = RB[0]
    for k in range(1, n_lon):
        total = total + RB[k]
    LB[lat] = total

    def lat_copy(d):
        return pltpu.make_async_remote_copy(
            src_ref=LB.at[lat], dst_ref=LB.at[lat], send_sem=ls_s.at[d], recv_sem=ls_r.at[d],
            device_id=(lon, lax.rem(lat + d, n_lat)), device_id_type=MESH,
        )

    for d in range(1, n_lat):
        lat_copy(d).start()
    for d in range(1, n_lat):
        lat_copy(d).wait_recv()
    total = LB[0]
    for k in range(1, n_lat):
        total = total + LB[k]
    wg_out[...] = total

    for d in range(1, n_lat):
        lat_copy(d).wait_send()

    @pl.loop(1, n_lon)
    def _(d):
        rows_copy(lax.rem(lon + d, n_lon), d, lon).wait_send()

    @pl.when(jnp.logical_not(top))
    def _():
        to_north.wait_send()
        to_nw.wait_send()

    @pl.when(top)
    def _():
        @pl.loop(1, n_lon)
        def _(d):
            fold_copy(lax.rem(lon + d, n_lon), d, lon).wait_send()

    @pl.when(jnp.logical_not(bottom))
    def _():
        to_south.wait_send()
        to_se.wait_send()

    to_east.wait_send()
    to_west.wait_send()
    wp_copy.wait()

    @pl.loop(0, n8)
    def _(i):
        pltpu.make_async_copy(GR.at[i], gr_out.at[i], gsem.at[i]).wait()


def feature_kernel(gr, wp, out):
    out[...] = lax.dot_general(
        gr[0], wp[...], (((0,), (0,)), ((), ())), preferred_element_type=F32
    ).astype(BF16)


def per_device(n_lon, n_lat, features, head_weight, target, metrics, masks, partner):
    R, C, ft = features.shape
    ch = target.shape[0]
    blk = ft // n_lon
    n8 = R // 8
    cells = R * C
    hbm = pl.BlockSpec(memory_space=pl.ANY)
    vmem = pl.BlockSpec(memory_space=pltpu.VMEM)
    V = pltpu.VMEM
    D = pltpu.SemaphoreType.DMA
    gr, wp, wg = pl.pallas_call(
        grads_kernel,
        out_shape=(
            jax.ShapeDtypeStruct((n8, CHP, 8 * C), BF16),
            jax.ShapeDtypeStruct((CHP, ft), BF16),
            jax.ShapeDtypeStruct((blk, C), F32),
        ),
        in_specs=[hbm] * 6,
        out_specs=(hbm, hbm, vmem),
        scratch_shapes=[
            V((cells, ft), BF16),
            V((ch, R, C), BF16),
            V(((ch + 4) * R, C), F32),
            V((6, R, C), F32),
            V((4, R, C), jnp.int32),
            V((ft, ch), BF16),
            V((n_lon, C), jnp.int32),
            V((CHP, ft), BF16),
            V(((R + 2) * ROW, C), F32),
            V((ROW, C), F32),
            V((ROW, C), F32),
            V((ROW, C), F32),
            V((32, C), F32),
            V((32, C), F32),
            V((24, C), F32),
            V((24, C), F32),
            V((n_lon, 24, C), F32),
            V((n8, CHP, 8 * C), BF16),
            V((CHP, ft), F32),
            V((ft, C), F32),
            V((n_lon, blk, C), F32),
            V((n_lat, blk, C), F32),
            D((R // 16,)), D((6,)), D((n8,)), D((6,)), D((6,)),
            D((n_lon,)), D((n_lon,)), D((n_lon,)), D((n_lon,)), D((n_lat,)), D((n_lat,)),
        ],
        compiler_params=pltpu.CompilerParams(
            collective_id=0, has_side_effects=True, vmem_limit_bytes=48 * 1024 * 1024
        ),
        cost_estimate=pl.CostEstimate(
            flops=4 * cells * ft * CHP, bytes_accessed=12 * 1024 * 1024, transcendentals=0
        ),
        name="grads_and_weight_grad",
    )(
        features.reshape(cells, ft), target, metrics, masks, head_weight,
        partner.reshape(n_lon, C),
    )
    feature_grad = pl.pallas_call(
        feature_kernel,
        grid=(n8,),
        out_shape=jax.ShapeDtypeStruct((cells, ft), BF16),
        in_specs=[
            pl.BlockSpec((1, CHP, 8 * C), lambda i: (i, 0, 0)),
            pl.BlockSpec((CHP, ft), lambda i: (0, 0)),
        ],
        out_specs=pl.BlockSpec((8 * C, ft), lambda i: (i, 0)),
        compiler_params=pltpu.CompilerParams(vmem_limit_bytes=32 * 1024 * 1024),
        cost_estimate=pl.CostEstimate(
            flops=2 * cells * ft * CHP, bytes_accessed=10 * 1024 * 1024, transcendentals=0
        ),
        name="feature_grad",
    )(gr, wp)
    weight_grad = jnp.concatenate([wg[:, 0:19], wg[:, 24:43], wg[:, 48:86]], axis=1)
    return feature_grad.reshape(R, C, ft), weight_grad


def solution(mesh):
    return jax.shard_map(
        functools.partial(per_device, mesh.shape["lon"], mesh.shape["lat"]),
        mesh=mesh,
        in_specs=(
            P("lat", "lon", None),
            P(),
            P(None, "lat", "lon"),
            P(None, "lat", "lon"),
            P(None, "lat", "lon"),
            P(),
        ),
        out_specs=(P("lat", "lon", None), P("lon", None)),
        check_vma=False,
    )
```

time: 423 us -> 50 us (0.12)
  blocking collectives: 168 us -> 0 us
  waiting for transfers between devices: 140 us -> 0 us
  Pallas kernels: 0 us -> 43.4 us
  starting transfers between devices: 39.9 us -> 0 us
  local copies, waits for them, and re-layouts: 26.9 us -> 5.01 us
  matrix products: 17 us -> 0 us
  other arithmetic: 16.3 us -> 0.68 us
  between operations: 14.3 us -> 0.65 us
    unnamed x2 -> x0, waiting for transfers between devices: 140 us -> none
    all_gather x2 -> x0, blocking collectives: 128 us -> none  [fold_row(): return lax.all_gather(top_row, 'lon', axis=1, tiled=True)]
    pallas_call x0 -> x2, Pallas kernels: none -> 43.4 us  [the longest x1 37.2 us: per_device(): pl.pallas_call(grads_kernel, out_shape=(jax.ShapeDtypeStruct((n8, CHP, 8...]
    ppermute x8 -> x0, starting transfers between devices: 39.9 us -> none  [the longest x4 23.9 us: padded(): lax.ppermute(lax.slice_in_dim(block, block.shape[dim] - width, None, axis...]
    psum x1 -> x0, blocking collectives: 39.4 us -> none  [per_device(): weight_grad = lax.psum(lon_rows, 'lat')]
    dot_general x3 -> x0, matrix products: 17 us -> none  [the longest x1 6.33 us: per_device(): lax.dot_general(head_weight, cell_rows, contract, preferred_element_type=...]
    slice x9 -> x2, local copies, waits for them, and re-layouts: 7.87 us -> 0.14 us  [the longest x1 0.07 us: per_device(): wg[:, 48:86]]
    ppermute x4 -> x0, local copies, waits for them, and re-layouts: 6.68 us -> none  [the longest x2 3.81 us: padded(): lax.ppermute(lax.slice_in_dim(block, block.shape[dim] - width, None, axis...]
  transfers between devices with their start and end apart: 9 -> 0, of which waited for: 1 -> 0; matrix products, arithmetic and copies ran while one was open for 8% -> 0% of each run, Pallas kernels for 0% -> 0%
where the time goes in v1:
time: 50 us; the launch traced here: 49.8 us
  Pallas kernels  43.4 us (87%)
  local copies, waits for them, and re-layouts  5.01 us (10%)
  other arithmetic  0.68 us (1%)
  between operations  0.65 us (1%)
    pallas_call x1, Pallas kernels, per_device(): pl.pallas_call(grads_kernel, out_shape=(jax.ShapeDtypeStruct((n8, CHP, 8...  37.2 us
    pallas_call x1, Pallas kernels, per_device(): pl.pallas_call(feature_kernel, grid=(n8,), out_shape=jax.ShapeDtypeStruct...  6.21 us
    unnamed x9, local copies, waits for them, and re-layouts  4.86 us

profile of v1, /device:TPU:1, one launch (start us, length us, event | category | flops | bytes accessed | tf_op | source)
XLA Modules:
  0.0 49.8 jit_solution(15125744590381025560)
XLA Ops:
  0.6 1.0 %copy.8.wt = bf16[512,76]{1,0:T(8,128)(2,1)S(1)} copy(bf16[512,76]{0,1:T(8,128)(2,1)} %param.7) | data formatting | bytes 155648 | tf_op args[1]
  1.7 0.0 copy-start
  1.7 1.3 %copy-done = bf16[76,64,128]{2,1,0:T(8,128)(2,1)S(1)} copy-done((bf16[76,64,128]{2,1,0:T(8,128)(2,1)S(1)}, bf16[76,64,128]{2,1,0:T(8,128)(2,1)}, u32[]{:S(2)}) %copy-start) | copy-done | bytes 1245208
  3.0 0.0 copy-start.1
  3.0 0.9 %copy-done.1 = f32[6,64,128]{2,1,0:T(8,128)S(1)} copy-done((f32[6,64,128]{2,1,0:T(8,128)S(1)}, f32[6,64,128]{2,1,0:T(8,128)}, u32[]{:S(2)}) %copy-start.1) | copy-done | bytes 196632
  3.9 0.0 copy-start.2
  3.9 0.9 %copy-done.2 = s32[4,64,128]{2,1,0:T(8,128)S(1)} copy-done((s32[4,64,128]{2,1,0:T(8,128)S(1)}, s32[4,64,128]{2,1,0:T(8,128)}, u32[]{:S(2)}) %copy-start.2) | copy-done | bytes 131096
  4.8 0.0 copy-start.3
  4.8 0.7 %copy-done.3 = s32[4096]{0:T(1024)S(1)} copy-done((s32[4096]{0:T(1024)S(1)}, s32[4096]{0:T(1024)}, u32[]{:S(2)}) %copy-start.3) | copy-done | bytes 16408
  5.5 37.2 %grads_and_weight_grad.1 = (bf16[8,96,1024]{2,1,0:T(8,128)(2,1)S(1)}, bf16[96,512]{1,0:T(8,128)(2,1)S(1)}, f32[16,128]{1,0:T(8,128)S(1)}) custom-call(bf16[8192,512]{1,0:T(8,128)(2,1)} %bitcast.4, bf16[76,64,128]{2,1,0:T(8,128)(2,1)S(1)} %copy-done, f32[6,64,128]{2,1,0:T(8,128)S(1)} %copy-done.1, s32[4,64,128]{2,1,0:T(8,128)S(1)} %copy-done.2, ...), custom_call_target="tpu_custom_call" | custom-call | flops 1610612736 | bytes 12582912 | tf_op jit(solution)/shard_map/grads_and_weight_grad/pallas_call | solution.py:414
  42.7 0.1 slice.11
  42.8 0.1 fusion
  42.9 0.7 %pad_maximum_fusion = f32[16,76]{1,0:T(8,128)} fusion(f32[16,38]{1,0:T(8,128)S(1)} %slice.11, f32[16,19]{1,0:T(8,128)S(1)} %get-tuple-element.9, f32[16,19]{1,0:T(8,128)S(1)} %get-tuple-element.8), kind=kLoop, calls=%fused_computation | loop fusion | flops 2432 | bytes 9728 | tf_op jit(solution)/shard_map/concatenate | solution.py:475
  43.6 6.2 %feature_grad.1 = bf16[8192,512]{1,0:T(8,128)(2,1)} custom-call(bf16[8,96,1024]{2,1,0:T(8,128)(2,1)S(1)} %get-tuple-element.5.gr, bf16[96,512]{1,0:T(8,128)(2,1)S(1)} %get-tuple-element.6.wp), custom_call_target="tpu_custom_call" | custom-call | flops 805306368 | bytes 10485760 | tf_op jit(solution)/shard_map/feature_grad/pallas_call | solution.py:460
Async XLA Ops:
  1.7 1.3 %copy-start = (bf16[76,64,128]{2,1,0:T(8,128)(2,1)S(1)}, bf16[76,64,128]{2,1,0:T(8,128)(2,1)}, u32[]{:S(2)}) copy-start(bf16[76,64,128]{2,1,0:T(8,128)(2,1)} %tgt.1) | copy-start | bytes 3735556
  3.0 0.9 %copy-start.1 = (f32[6,64,128]{2,1,0:T(8,128)S(1)}, f32[6,64,128]{2,1,0:T(8,128)}, u32[]{:S(2)}) copy-start(f32[6,64,128]{2,1,0:T(8,128)} %met.1) | copy-start | bytes 589828
  3.9 0.9 %copy-start.2 = (s32[4,64,128]{2,1,0:T(8,128)S(1)}, s32[4,64,128]{2,1,0:T(8,128)}, u32[]{:S(2)}) copy-start(s32[4,64,128]{2,1,0:T(8,128)} %msk.1) | copy-start | bytes 393220
  4.8 0.7 %copy-start.3 = (s32[4096]{0:T(1024)S(1)}, s32[4096]{0:T(1024)}, u32[]{:S(2)}) copy-start(s32[4096]{0:T(1024)} %param.11) | copy-start | bytes 49156

commit v2 on v1

--- a/solution.py
+++ b/solution.py
@@ -14,6 +14,7 @@
 F32 = jnp.float32
 BF16 = jnp.bfloat16
 NT = (((1,), (1,)), ((), ()))
+NN = (((1,), (0,)), ((), ()))
 
 
 def lanes(shape):
@@ -22,18 +23,14 @@
 
 def grads_kernel(
     feat, tgt, met, msk, wt, part, gr_out, wp_out, wg_out,
-    F, Tb, Tf, M, K, Wv, Pv, Wp, EG, ED, HW, HE, CNW, CSE, CW, FS, FB, GR, ACC, WS, RB, LB,
-    fsem, lsem, gsem, hs, hr, fs_s, fs_r, rs_s, rs_r, ls_s, ls_r,
+    F, Tb, Tf, M, K, Wv, Pv, Wp, EG, ED, FE, HW, HE, CNW, CSE, CW, FS, FB, GR, ACC, WS, RB, LB,
+    fsem, esem, lsem, gsem, hs, hr, fs_s, fs_r, rs_s, rs_r, ls_s, ls_r,
 ):
     n_lon, n_lat = lax.axis_size("lon"), lax.axis_size("lat")
     lon, lat = lax.axis_index("lon"), lax.axis_index("lat")
-    R = tgt.shape[1]
-    C = tgt.shape[2]
-    ft = feat.shape[1]
+    R, C, ft = feat.shape
     n16 = R // 16
     n8 = R // 8
-    cells16 = 16 * C
-    cells8 = 8 * C
     blk = ft // n_lon
     top = lat == n_lat - 1
     bottom = lat == 0
@@ -42,9 +39,23 @@
     up = lax.rem(lat + 1, n_lat)
     down = lax.rem(lat + n_lat - 1, n_lat)
 
+    barrier = pltpu.get_barrier_semaphore()
+    pl.semaphore_signal(barrier, inc=1, device_id=(east, lat), device_id_type=MESH)
+    pl.semaphore_signal(barrier, inc=1, device_id=(west, lat), device_id_type=MESH)
+    for d in range(1, n_lat):
+        pl.semaphore_signal(
+            barrier, inc=1, device_id=(lon, lax.rem(lat + d, n_lat)), device_id_type=MESH
+        )
+    pl.semaphore_signal(barrier, inc=1, device_id=(east, down), device_id_type=MESH)
+    pl.semaphore_signal(barrier, inc=1, device_id=(west, up), device_id_type=MESH)
+
     def fcopy(c):
-        at = pl.ds(pl.multiple_of(c * cells16, cells16), cells16)
+        at = (pl.ds(pl.multiple_of(c * 16, 16), 16), pl.ds(16, C - 32))
         return pltpu.make_async_copy(feat.at[at], F.at[at], fsem.at[c])
+
+    def ecopy(k):
+        at = (pl.ds(0, R), pl.ds(k * (C - 16), 16))
+        return pltpu.make_async_copy(feat.at[at], F.at[at], esem.at[k])
 
     small = [
         pltpu.make_async_copy(met, M, lsem.at[0]),
@@ -55,6 +66,8 @@
     ]
     for copy in small:
         copy.start()
+    ecopy(0).start()
+    ecopy(1).start()
     for i in range(n16):
         fcopy((i + n16 - 1) % n16).start()
 
@@ -68,20 +81,11 @@
         EG[(R + 1) * ROW : (R + 2) * ROW, :] = jnp.zeros((ROW, C), F32)
         CNW[...] = jnp.zeros_like(CNW)
 
-    barrier = pltpu.get_barrier_semaphore()
-
-    @pl.loop(1, n_lon)
+    @pl.loop(2, n_lon - 1)
     def _(d):
         pl.semaphore_signal(
             barrier, inc=1, device_id=(lax.rem(lon + d, n_lon), lat), device_id_type=MESH
         )
-
-    for d in range(1, n_lat):
-        pl.semaphore_signal(
-            barrier, inc=1, device_id=(lon, lax.rem(lat + d, n_lat)), device_id_type=MESH
-        )
-    pl.semaphore_signal(barrier, inc=1, device_id=(east, down), device_id_type=MESH)
-    pl.semaphore_signal(barrier, inc=1, device_id=(west, up), device_id_type=MESH)
 
     small[0].wait()
     small[1].wait()
@@ -101,18 +105,72 @@
     small[2].wait()
     p = lax.broadcasted_iota(jnp.int32, (CHP, 4 * LEV), 0)
     c = lax.broadcasted_iota(jnp.int32, (CHP, 4 * LEV), 1)
-    pick = ((p < 19) & (c == p)) | ((p >= 24) & (p < 43) & (c == p - 5))
-    pick = pick | ((p >= 48) & (p < 86) & (c == p - 10))
+    level = (p // 16) * 8 + p % 8
+    pick = (p < 48) & (level < LEV) & (c == level + LEV * ((p // 8) % 2))
+    pick = pick | ((p >= 48) & (c == p - 10))
     wp = lax.dot_general(
-        jnp.where(pick, 1.0, 0.0).astype(BF16), Wv[...], NT, preferred_element_type=F32
+        jnp.where(pick, 1.0, 0.0).astype(BF16), Wv[...], NN, preferred_element_type=F32
     )
     Wp[...] = wp.astype(BF16)
     wp_copy = pltpu.make_async_copy(Wp, wp_out, lsem.at[5])
     wp_copy.start()
-    ED[...] = jnp.zeros_like(ED)
     Tf[4 * LEV * R :, :] = jnp.zeros((4 * R, C), F32)
     small[3].wait()
     small[4].wait()
+
+    def true_at(first, r):
+        return Tf[pl.ds(first * R + r, 8, stride=R), :]
+
+    def widen(i, _):
+        at = pl.multiple_of(16 * i, 16)
+        for ch in range(4 * LEV):
+            Tf[pl.ds(pl.multiple_of(ch * R + at, 16), 16), :] = Tb[ch, pl.ds(at, 16), :].astype(F32)
+        return 0
+
+    lax.fori_loop(0, n16, widen, 0)
+
+    half = lanes((8, C)) >> 1
+
+    def pack(i, packed):
+        packed = list(packed)
+        for j in range(16):
+            r = 16 * i + j
+            base = pl.multiple_of((r + 1) * ROW, 8)
+            rows = [true_at(8 * k, r) for k in range(3)]
+            rows.append(EG[pl.ds(base + 24, 8), :])
+            rows += [true_at(LEV + 8 * k, r) for k in range(3)]
+            by = 2 * r + 1
+            packed = [
+                jnp.where(half == r, pltpu.roll(x, by, 1), y) for x, y in zip(rows, packed)
+            ]
+        return tuple(packed)
+
+    zero8 = jnp.zeros((8, C), F32)
+    packed = lax.fori_loop(0, n16, pack, (zero8,) * 7)
+    q = lax.broadcasted_iota(jnp.int32, (32, 512), 0)
+    cell = lax.broadcasted_iota(jnp.int32, (32, 512), 1)
+    row16 = (q >> 1) * 16
+    wanted = row16 + jnp.where((q & 1) == 1, 0, 256 + 15)
+    choose = jnp.where(cell == wanted, 1.0, 0.0).astype(BF16)
+    ecopy(0).wait()
+    ecopy(1).wait()
+    for i in range(n16):
+        rows = slice(16 * i, 16 * i + 16)
+        both = jnp.concatenate(
+            [F[rows, 0:16, :].reshape(256, ft), F[rows, C - 16 : C, :].reshape(256, ft)], 0
+        )
+        FE[32 * i : 32 * i + 32, :] = jnp.dot(
+            choose, both, preferred_element_type=F32
+        ).astype(BF16)
+    at_edges = lax.dot_general(Wp[0:48, :], FE[...], NT, preferred_element_type=F32)
+    for k in range(3):
+        ED[8 * k : 8 * k + 8, 0 : 2 * R] = (
+            at_edges[16 * k : 16 * k + 8] - packed[k][:, 0 : 2 * R]
+        )
+        ED[32 + 8 * k : 40 + 8 * k, 0 : 2 * R] = (
+            at_edges[16 * k + 8 : 16 * k + 16] - packed[4 + k][:, 0 : 2 * R]
+        )
+    ED[24:32, :] = packed[3]
 
     def send(src, dst, k, device):
         return pltpu.make_async_remote_copy(
@@ -141,38 +199,29 @@
         chunk = lax.rem(i + n16 - 1, n16)
         r0 = pl.multiple_of(chunk * 16, 16)
         fcopy(chunk).wait()
-        for ch in range(4 * LEV):
-            at = pl.ds(pl.multiple_of(ch * R + r0, 16), 16)
-            Tf[at, :] = Tb[ch, pl.ds(r0, 16), :].astype(F32)
-        half = lanes((ROW, C)) >> 1
-        packed = ED[...]
         for j4 in range(4):
-            cells = pl.ds(pl.multiple_of(chunk * cells16 + j4 * 4 * C, 4 * C), 4 * C)
-            predicted = lax.dot_general(Wp[...], F[cells, :], NT, preferred_element_type=F32)
+            cells = F[pl.ds(r0 + 4 * j4, 4), :, :].reshape(4 * C, ft)
+            predicted = lax.dot_general(Wp[...], cells, NT, preferred_element_type=F32)
             for j in range(4):
-                r = r0 + 4 * j4 + j
+                q = 4 * j4 + j
+                r = r0 + q
                 base = pl.multiple_of((r + 1) * ROW, 8)
                 mine = predicted[:, j * C : (j + 1) * C]
-
-                def true_at(first, count):
-                    return jnp.concatenate(
-                        [Tf[pl.ds((first + 8 * k) * R + r, 8, stride=R), :] for k in range(count)], 0
+                for k in range(3):
+                    EG[pl.ds(base + 8 * k, 8), :] = mine[16 * k : 16 * k + 8] - true_at(8 * k, r)
+                    EG[pl.ds(base + 32 + 8 * k, 8), :] = (
+                        mine[16 * k + 8 : 16 * k + 16] - true_at(LEV + 8 * k, r)
                     )
-
-                EG[pl.ds(base, 24), :] = mine[0:24] - true_at(0, 3)
-                EG[pl.ds(base + 32, 24), :] = mine[24:48] - true_at(LEV, 3)
-                other = (mine[48:88] - true_at(2 * LEV, 5)) * EG[pl.ds(base + 30, 1), :]
+                other = [mine[48 + 8 * k : 56 + 8 * k] - true_at(2 * LEV + 8 * k, r) for k in range(5)]
+                other = jnp.concatenate(other, 0) * EG[pl.ds(base + 30, 1), :]
                 other = jnp.concatenate([other, jnp.zeros((8, C), F32)], 0)
-                q = 4 * j4 + j
-                GR[2 * chunk + q // 8, 48:CHP, (q % 8) * C : (q % 8 + 1) * C] = other.astype(BF16)
-                packed = jnp.where(
-                    half == r, pltpu.roll(EG[pl.ds(base, ROW), :], 2 * r + 1, 1), packed
-                )
-        ED[...] = packed
+                GR[2 * chunk + q // 8 + 1, 48:CHP, (q % 8) * C : (q % 8 + 1) * C] = other.astype(BF16)
 
         @pl.when(i == 0)
         def _():
             pl.semaphore_wait(barrier, n_lon + n_lat)
+            to_east.start()
+            to_west.start()
 
             @pl.when(jnp.logical_not(top))
             def _():
@@ -202,8 +251,6 @@
         return 0
 
     lax.fori_loop(0, n16, errors_chunk, 0)
-    to_east.start()
-    to_west.start()
 
     @pl.when(jnp.logical_not(bottom))
     def _():
@@ -233,33 +280,44 @@
     edge_a = jnp.where(even, flux_e, across_w)
     edge_b = jnp.where(even, tension_e, summed_w)
 
-    def u_at(base):
-        return EG[pl.ds(base, 24), :]
-
-    def v_at(base):
-        return EG[pl.ds(base + 32, 24), :]
+    lane8 = lanes((8, C))
+
+    def u_at(base, g):
+        return EG[pl.ds(base + 8 * g, 8), :]
+
+    def v_at(base, g):
+        return EG[pl.ds(base + 32 + 8 * g, 8), :]
 
     def coef(base, k):
         return EG[pl.ds(base + 24 + k, 1), :]
 
     def shifted_west(x, edge):
-        return jnp.where(lane == 0, edge, roll(x, 1))
+        return jnp.where(lane8 == 0, edge, roll(x, 1))
 
     def shifted_east(x, edge):
-        return jnp.where(lane == C - 1, edge, roll(x, C - 1))
-
-    uf0 = u_at(ROW) * coef(ROW, 0)
-    va0 = v_at(ROW) * coef(ROW, 3)
-    ra0 = roll(edge_a, C - 1)
-    ua0 = u_at(ROW) * coef(ROW, 1)
-    ct0 = coef(ROW, 5) * (ua0 - shifted_west(ua0, ra0) - va0 + v_at(0) * coef(0, 3))
-    df0 = coef(0, 7) * (u_at(0) * coef(0, 0) - uf0)
+        return jnp.where(lane8 == C - 1, edge, roll(x, C - 1))
+
+    first = []
+    for g in range(3):
+        uf0 = u_at(ROW, g) * coef(ROW, 0)
+        va0 = v_at(ROW, g) * coef(ROW, 3)
+        ra0 = roll(edge_a[8 * g : 8 * g + 8], C - 1)
+        ua0 = u_at(ROW, g) * coef(ROW, 1)
+        before = v_at(0, g) * coef(0, 3)
+        ct0 = coef(ROW, 5) * (ua0 - shifted_west(ua0, ra0) - va0 + before)
+        df0 = coef(0, 7) * (u_at(0, g) * coef(0, 0) - uf0)
+        first.append((uf0, va0, ct0, df0, ra0))
 
     ACC[...] = jnp.zeros_like(ACC)
     CW[...] = jnp.zeros_like(CW)
 
+    GR[0] = jnp.zeros(GR.shape[1:], BF16)
+
+    def weight_chunk(slot, chunk):
+        cells = F[pl.ds(pl.multiple_of(8 * chunk, 8), 8), :, :].reshape(8 * C, ft)
+        ACC[...] += jnp.dot(GR[slot], cells, preferred_element_type=F32)
+
     def stencil_chunk(i, carry):
-        uf, va, ct, df, ra = carry
         last = i == n8 - 1
 
         @pl.when(last)
@@ -293,32 +351,39 @@
                 at = R * ROW + 31
                 EG[at : at + 1, :] = EG[at : at + 1, :] + found[23:24]
 
-        for j in range(8):
-            r = 8 * i + j
-            b0 = pl.multiple_of((r + 1) * ROW, 8)
-            b1 = pl.multiple_of((r + 2) * ROW, 8)
-            u1, v1 = u_at(b1), v_at(b1)
-            uf1, ua1, va1 = u1 * coef(b1, 0), u1 * coef(b1, 1), v1 * coef(b1, 3)
-            ra1 = roll(edge_a, lax.rem(4 * C - 3 - 2 * r, C))
-            if j == 7:
-                ra1 = jnp.where(last, CW[...], ra1)
-            rb = roll(edge_b, C - 1 - 2 * r)
-            df1 = coef(b0, 7) * (uf - uf1)
-            ct1 = coef(b1, 5) * (ua1 - shifted_west(ua1, ra1) - va1 + va)
-            vf = v_at(b0) * coef(b0, 2)
-            summed = coef(b0, 4) * (shifted_east(vf, ra) - vf)
-            grad_v = shifted_west(summed, rb) - summed
-            grad_uy = ct - shifted_east(ct, rb)
-            gu = coef(b0, 0) * (df1 - df) + coef(b0, 1) * grad_uy
-            gv = coef(b0, 2) * grad_v + coef(b0, 3) * (ct1 - ct)
-            GR[i, 0:48, j * C : (j + 1) * C] = jnp.concatenate([gu, gv], 0).astype(BF16)
-            uf, va, ct, df, ra = uf1, va1, ct1, df1, ra1
-        pltpu.make_async_copy(GR.at[i], gr_out.at[i], gsem.at[i]).start()
-        cells = pl.ds(pl.multiple_of(i * cells8, cells8), cells8)
-        ACC[...] += jnp.dot(GR[i], F[cells, :], preferred_element_type=F32)
-        return uf, va, ct, df, ra
-
-    lax.fori_loop(0, n8, stencil_chunk, (uf0, va0, ct0, df0, ra0))
+        weight_chunk(i, jnp.maximum(i - 1, 0))
+        after = []
+        for g in range(3):
+            uf, va, ct, df, ra = carry[g]
+            mine_a = edge_a[8 * g : 8 * g + 8]
+            mine_b = edge_b[8 * g : 8 * g + 8]
+            for j in range(8):
+                r = 8 * i + j
+                b0 = pl.multiple_of((r + 1) * ROW, 8)
+                b1 = pl.multiple_of((r + 2) * ROW, 8)
+                u1, v1 = u_at(b1, g), v_at(b1, g)
+                uf1, ua1, va1 = u1 * coef(b1, 0), u1 * coef(b1, 1), v1 * coef(b1, 3)
+                ra1 = roll(mine_a, lax.rem(4 * C - 3 - 2 * r, C))
+                if j == 7:
+                    ra1 = jnp.where(last, CW[8 * g : 8 * g + 8, :], ra1)
+                rb = roll(mine_b, C - 1 - 2 * r)
+                df1 = coef(b0, 7) * (uf - uf1)
+                ct1 = coef(b1, 5) * (ua1 - shifted_west(ua1, ra1) - va1 + va)
+                vf = v_at(b0, g) * coef(b0, 2)
+                summed = coef(b0, 4) * (shifted_east(vf, ra) - vf)
+                grad_v = shifted_west(summed, rb) - summed
+                grad_uy = ct - shifted_east(ct, rb)
+                gu = coef(b0, 0) * (df1 - df) + coef(b0, 1) * grad_uy
+                gv = coef(b0, 2) * grad_v + coef(b0, 3) * (ct1 - ct)
+                GR[i + 1, 16 * g : 16 * g + 16, j * C : (j + 1) * C] = jnp.concatenate(
+                    [gu, gv], 0
+                ).astype(BF16)
+                uf, va, ct, df, ra = uf1, va1, ct1, df1, ra1
+            after.append((uf, va, ct, df, ra))
+        return tuple(after)
+
+    lax.fori_loop(0, n8, stencil_chunk, tuple(first))
+    weight_chunk(n8, n8 - 1)
 
     scale = 1.0 / (R * n_lat * C * n_lon)
     acc = ACC[...] * scale
@@ -335,6 +400,10 @@
     @pl.loop(1, n_lon)
     def _(d):
         rows_copy(lax.rem(lon + d, n_lon), d, lon).start()
+
+    @pl.loop(0, n8)
+    def _(i):
+        pltpu.make_async_copy(GR.at[i + 1], gr_out.at[i], gsem.at[i]).start()
 
     RB[lon] = WS[pl.ds(pl.multiple_of(lon * blk, blk), blk), :]
 
@@ -361,7 +430,9 @@
     total = LB[0]
     for k in range(1, n_lat):
         total = total + LB[k]
-    wg_out[...] = total
+    pieces = [total[:, 16 * g : 16 * g + 8] for g in range(2)] + [total[:, 32:35]]
+    pieces += [total[:, 16 * g + 8 : 16 * g + 16] for g in range(2)] + [total[:, 40:43]]
+    wg_out[...] = jnp.concatenate(pieces + [total[:, 48:86]], 1)
 
     for d in range(1, n_lat):
         lat_copy(d).wait_send()
@@ -392,13 +463,25 @@
 
     @pl.loop(0, n8)
     def _(i):
-        pltpu.make_async_copy(GR.at[i], gr_out.at[i], gsem.at[i]).wait()
-
-
-def feature_kernel(gr, wp, out):
-    out[...] = lax.dot_general(
-        gr[0], wp[...], (((0,), (0,)), ((), ())), preferred_element_type=F32
-    ).astype(BF16)
+        pltpu.make_async_copy(GR.at[i + 1], gr_out.at[i], gsem.at[i]).wait()
+
+
+def feature_kernel(gr, wp, out, held, sems):
+    pieces, ft = sems.shape[0], held.shape[1]
+    per = held.shape[0] // pieces
+    in_slot = gr.shape[2] // per
+    copies = []
+    for i in range(pieces):
+        at = slice(i * per, (i + 1) * per)
+        cells = slice(i % in_slot * per, (i % in_slot + 1) * per)
+        held[at, :] = lax.dot_general(
+            gr[i // in_slot, :, cells], wp[...], (((0,), (0,)), ((), ())),
+            preferred_element_type=F32,
+        ).astype(BF16)
+        copies.append(pltpu.make_async_copy(held.at[at], out.at[at], sems.at[i]))
+        copies[-1].start()
+    for copy in copies:
+        copy.wait()
 
 
 def per_device(n_lon, n_lat, features, head_weight, target, metrics, masks, partner):
@@ -416,21 +499,22 @@
         out_shape=(
             jax.ShapeDtypeStruct((n8, CHP, 8 * C), BF16),
             jax.ShapeDtypeStruct((CHP, ft), BF16),
-            jax.ShapeDtypeStruct((blk, C), F32),
+            jax.ShapeDtypeStruct((blk, ch), F32),
         ),
-        in_specs=[hbm] * 6,
+        in_specs=[pl.BlockSpec(memory_space=pltpu.HBM)] * 6,
         out_specs=(hbm, hbm, vmem),
         scratch_shapes=[
-            V((cells, ft), BF16),
+            V((R, C, ft), BF16),
             V((ch, R, C), BF16),
             V(((ch + 4) * R, C), F32),
             V((6, R, C), F32),
             V((4, R, C), jnp.int32),
-            V((ft, ch), BF16),
+            V((ch, ft), BF16),
             V((n_lon, C), jnp.int32),
             V((CHP, ft), BF16),
             V(((R + 2) * ROW, C), F32),
             V((ROW, C), F32),
+            V((2 * R, ft), BF16),
             V((ROW, C), F32),
             V((ROW, C), F32),
             V((32, C), F32),
@@ -438,12 +522,12 @@
             V((24, C), F32),
             V((24, C), F32),
             V((n_lon, 24, C), F32),
-            V((n8, CHP, 8 * C), BF16),
+            V((n8 + 1, CHP, 8 * C), BF16),
             V((CHP, ft), F32),
             V((ft, C), F32),
             V((n_lon, blk, C), F32),
             V((n_lat, blk, C), F32),
-            D((R // 16,)), D((6,)), D((n8,)), D((6,)), D((6,)),
+            D((R // 16,)), D((2,)), D((6,)), D((n8,)), D((6,)), D((6,)),
             D((n_lon,)), D((n_lon,)), D((n_lon,)), D((n_lon,)), D((n_lat,)), D((n_lat,)),
         ],
         compiler_params=pltpu.CompilerParams(
@@ -454,26 +538,27 @@
         ),
         name="grads_and_weight_grad",
     )(
-        features.reshape(cells, ft), target, metrics, masks, head_weight,
-        partner.reshape(n_lon, C),
+        *(
+            pltpu.with_memory_space_constraint(x, pltpu.HBM)
+            for x in (
+                features, target, metrics, masks, head_weight.T,
+                partner.reshape(n_lon, C),
+            )
+        )
     )
     feature_grad = pl.pallas_call(
         feature_kernel,
-        grid=(n8,),
         out_shape=jax.ShapeDtypeStruct((cells, ft), BF16),
-        in_specs=[
-            pl.BlockSpec((1, CHP, 8 * C), lambda i: (i, 0, 0)),
-            pl.BlockSpec((CHP, ft), lambda i: (0, 0)),
-        ],
-        out_specs=pl.BlockSpec((8 * C, ft), lambda i: (i, 0)),
+        in_specs=[vmem, vmem],
+        out_specs=hbm,
+        scratch_shapes=[V((cells, ft), BF16), D((2 * n8,))],
         compiler_params=pltpu.CompilerParams(vmem_limit_bytes=32 * 1024 * 1024),
         cost_estimate=pl.CostEstimate(
             flops=2 * cells * ft * CHP, bytes_accessed=10 * 1024 * 1024, transcendentals=0
         ),
         name="feature_grad",
     )(gr, wp)
-    weight_grad = jnp.concatenate([wg[:, 0:19], wg[:, 24:43], wg[:, 48:86]], axis=1)
-    return feature_grad.reshape(R, C, ft), weight_grad
+    return feature_grad.reshape(R, C, ft), wg
 
 
 def solution(mesh):

time: 50 us -> 38.6 us (0.77)
  Pallas kernels: 43.4 us -> 37.3 us
  local copies, waits for them, and re-layouts: 5.01 us -> 0.6 us
  other arithmetic: 0.68 us -> 0 us
    unnamed x9 -> x1, local copies, waits for them, and re-layouts: 4.86 us -> 0.6 us
    pallas_call x1, Pallas kernels: 37.2 us -> 33.5 us  [per_device(): pl.pallas_call(grads_kernel, out_shape=(jax.ShapeDtypeStruct((n8, CHP, 8...]
    pallas_call x1, Pallas kernels: 6.21 us -> 3.74 us  [per_device(): pl.pallas_call(feature_kernel, out_shape=jax.ShapeDtypeStruct((cells, ft)...]
    concatenate x1 -> x0, other arithmetic: 0.68 us -> none  [per_device(): jnp.concatenate([wg[:, 0:19], wg[:, 24:43], wg[:, 48:86]], axis=1)]
where the time goes in v2:
time: 38.6 us; the launch traced here: 38.5 us
  Pallas kernels  37.3 us (97%)
  between operations  0.65 us (2%)
  local copies, waits for them, and re-layouts  0.6 us (2%)
    pallas_call x1, Pallas kernels, per_device(): pl.pallas_call(grads_kernel, out_shape=(jax.ShapeDtypeStruct((n8, CHP, 8...  33.5 us
    pallas_call x1, Pallas kernels, per_device(): pl.pallas_call(feature_kernel, out_shape=jax.ShapeDtypeStruct((cells, ft)...  3.74 us

profile of v2, /device:TPU:1, one launch (start us, length us, event | category | flops | bytes accessed | tf_op | source)
XLA Modules:
  0.0 38.5 jit_solution(13108215429816117371)
XLA Ops:
  0.6 33.5 %grads_and_weight_grad.1 = (bf16[8,96,1024]{2,1,0:T(8,128)(2,1)S(1)}, bf16[96,512]{1,0:T(8,128)(2,1)S(1)}, f32[16,76]{1,0:T(8,128)S(1)}) custom-call(bf16[64,128,512]{2,1,0:T(8,128)(2,1)} %feat.1, bf16[76,64,128]{2,1,0:T(8,128)(2,1)} %tgt.1, f32[6,64,128]{2,1,0:T(8,128)} %met.1, s32[4,64,128]{2,1,0:T(8,128)} %msk.1, bf16[76,512]{1,0:T(8,128)(2,1)} %bitcast.4, ...), custom_call_target="tpu_custom_call" | custom-call | flops 1610612736 | bytes 12582912 | tf_op jit(solution)/shard_map/grads_and_weight_grad/pallas_call | solution.py:497
  34.2 3.7 %feature_grad.1 = bf16[8192,512]{1,0:T(8,128)(2,1)} custom-call(bf16[8,96,1024]{2,1,0:T(8,128)(2,1)S(1)} %get-tuple-element.5.gr, bf16[96,512]{1,0:T(8,128)(2,1)S(1)} %get-tuple-element.6.wp), custom_call_target="tpu_custom_call" | custom-call | flops 805306368 | bytes 10485760 | tf_op jit(solution)/shard_map/feature_grad/pallas_call | solution.py:549
  37.9 0.6 %copy.9 = f32[16,76]{1,0:T(8,128)} copy(f32[16,76]{1,0:T(8,128)S(1)} %get-tuple-element.11) | data formatting | bytes 9728

commit v3 on v2

--- a/solution.py
+++ b/solution.py
@@ -23,8 +23,8 @@
 
 def grads_kernel(
     feat, tgt, met, msk, wt, part, gr_out, wp_out, wg_out,
-    F, Tb, Tf, M, K, Wv, Pv, Wp, EG, ED, FE, HW, HE, CNW, CSE, CW, FS, FB, GR, ACC, WS, RB, LB,
-    fsem, esem, lsem, gsem, hs, hr, fs_s, fs_r, rs_s, rs_r, ls_s, ls_r,
+    F, Tb, Tf, M, K, Wv, Pv, Wp, EG, ED, FE, DX, HW, HE, CNW, CSE, FS, FB, GR, ACC, WS, RB, LB,
+    fsem, lsem, gsem, hs, hr, fs_s, fs_r, rs_s, rs_r, ls_s, ls_r,
 ):
     n_lon, n_lat = lax.axis_size("lon"), lax.axis_size("lat")
     lon, lat = lax.axis_index("lon"), lax.axis_index("lat")
@@ -50,24 +50,18 @@
     pl.semaphore_signal(barrier, inc=1, device_id=(west, up), device_id_type=MESH)
 
     def fcopy(c):
-        at = (pl.ds(pl.multiple_of(c * 16, 16), 16), pl.ds(16, C - 32))
+        at = pl.ds(c * 16, 16)
         return pltpu.make_async_copy(feat.at[at], F.at[at], fsem.at[c])
-
-    def ecopy(k):
-        at = (pl.ds(0, R), pl.ds(k * (C - 16), 16))
-        return pltpu.make_async_copy(feat.at[at], F.at[at], esem.at[k])
 
     small = [
         pltpu.make_async_copy(met, M, lsem.at[0]),
         pltpu.make_async_copy(msk, K, lsem.at[1]),
         pltpu.make_async_copy(wt, Wv, lsem.at[2]),
         pltpu.make_async_copy(part, Pv, lsem.at[3]),
-        pltpu.make_async_copy(tgt, Tb, lsem.at[4]),
+        pltpu.make_async_copy(tgt, Tb.at[0 : 4 * LEV], lsem.at[4]),
     ]
     for copy in small:
         copy.start()
-    ecopy(0).start()
-    ecopy(1).start()
     for i in range(n16):
         fcopy((i + n16 - 1) % n16).start()
 
@@ -114,63 +108,26 @@
     Wp[...] = wp.astype(BF16)
     wp_copy = pltpu.make_async_copy(Wp, wp_out, lsem.at[5])
     wp_copy.start()
-    Tf[4 * LEV * R :, :] = jnp.zeros((4 * R, C), F32)
     small[3].wait()
+
+    firsts = [0, LEV, 8, LEV + 8, 16, LEV + 16] + [2 * LEV + 8 * k for k in range(5)]
+    Tb[4 * LEV :, :, :] = jnp.zeros((4, R, C), BF16)
     small[4].wait()
 
-    def true_at(first, r):
-        return Tf[pl.ds(first * R + r, 8, stride=R), :]
-
     def widen(i, _):
-        at = pl.multiple_of(16 * i, 16)
-        for ch in range(4 * LEV):
-            Tf[pl.ds(pl.multiple_of(ch * R + at, 16), 16), :] = Tb[ch, pl.ds(at, 16), :].astype(F32)
+        at = pl.ds(pl.multiple_of(16 * i, 16), 16)
+        for k, ch in enumerate(firsts):
+            turned = jnp.swapaxes(Tb[ch : ch + 8, at, :].astype(F32), 0, 1)
+            Tf[at, 8 * k : 8 * k + 8, :] = turned
         return 0
 
     lax.fori_loop(0, n16, widen, 0)
 
-    half = lanes((8, C)) >> 1
-
-    def pack(i, packed):
-        packed = list(packed)
-        for j in range(16):
-            r = 16 * i + j
-            base = pl.multiple_of((r + 1) * ROW, 8)
-            rows = [true_at(8 * k, r) for k in range(3)]
-            rows.append(EG[pl.ds(base + 24, 8), :])
-            rows += [true_at(LEV + 8 * k, r) for k in range(3)]
-            by = 2 * r + 1
-            packed = [
-                jnp.where(half == r, pltpu.roll(x, by, 1), y) for x, y in zip(rows, packed)
-            ]
-        return tuple(packed)
-
-    zero8 = jnp.zeros((8, C), F32)
-    packed = lax.fori_loop(0, n16, pack, (zero8,) * 7)
-    q = lax.broadcasted_iota(jnp.int32, (32, 512), 0)
-    cell = lax.broadcasted_iota(jnp.int32, (32, 512), 1)
-    row16 = (q >> 1) * 16
-    wanted = row16 + jnp.where((q & 1) == 1, 0, 256 + 15)
+    q = lax.broadcasted_iota(jnp.int32, (16, 256), 0)
+    cell = lax.broadcasted_iota(jnp.int32, (16, 256), 1)
+    wanted = (q >> 1) * 16 + jnp.where((q & 1) == 1, 0, 128 + 15)
     choose = jnp.where(cell == wanted, 1.0, 0.0).astype(BF16)
-    ecopy(0).wait()
-    ecopy(1).wait()
-    for i in range(n16):
-        rows = slice(16 * i, 16 * i + 16)
-        both = jnp.concatenate(
-            [F[rows, 0:16, :].reshape(256, ft), F[rows, C - 16 : C, :].reshape(256, ft)], 0
-        )
-        FE[32 * i : 32 * i + 32, :] = jnp.dot(
-            choose, both, preferred_element_type=F32
-        ).astype(BF16)
-    at_edges = lax.dot_general(Wp[0:48, :], FE[...], NT, preferred_element_type=F32)
-    for k in range(3):
-        ED[8 * k : 8 * k + 8, 0 : 2 * R] = (
-            at_edges[16 * k : 16 * k + 8] - packed[k][:, 0 : 2 * R]
-        )
-        ED[32 + 8 * k : 40 + 8 * k, 0 : 2 * R] = (
-            at_edges[16 * k + 8 : 16 * k + 16] - packed[4 + k][:, 0 : 2 * R]
-        )
-    ED[24:32, :] = packed[3]
+    ED[...] = jnp.zeros_like(ED)
 
     def send(src, dst, k, device):
         return pltpu.make_async_remote_copy(
@@ -195,33 +152,34 @@
             device_id=(peer, lat), device_id_type=MESH,
         )
 
+    half = lanes((ROW, C)) >> 1
+
     def errors_chunk(i, _):
-        chunk = lax.rem(i + n16 - 1, n16)
-        r0 = pl.multiple_of(chunk * 16, 16)
+        chunk = (i + n16 - 1) % n16
+        r0 = chunk * 16
         fcopy(chunk).wait()
+        packed = ED[...]
         for j4 in range(4):
             cells = F[pl.ds(r0 + 4 * j4, 4), :, :].reshape(4 * C, ft)
             predicted = lax.dot_general(Wp[...], cells, NT, preferred_element_type=F32)
             for j in range(4):
                 q = 4 * j4 + j
                 r = r0 + q
-                base = pl.multiple_of((r + 1) * ROW, 8)
-                mine = predicted[:, j * C : (j + 1) * C]
+                base = (r + 1) * ROW
+                mine = predicted[0:88, j * C : (j + 1) * C] - Tf[r]
                 for k in range(3):
-                    EG[pl.ds(base + 8 * k, 8), :] = mine[16 * k : 16 * k + 8] - true_at(8 * k, r)
-                    EG[pl.ds(base + 32 + 8 * k, 8), :] = (
-                        mine[16 * k + 8 : 16 * k + 16] - true_at(LEV + 8 * k, r)
-                    )
-                other = [mine[48 + 8 * k : 56 + 8 * k] - true_at(2 * LEV + 8 * k, r) for k in range(5)]
-                other = jnp.concatenate(other, 0) * EG[pl.ds(base + 30, 1), :]
+                    EG[pl.ds(base + 8 * k, 8), :] = mine[16 * k : 16 * k + 8]
+                    EG[pl.ds(base + 32 + 8 * k, 8), :] = mine[16 * k + 8 : 16 * k + 16]
+                other = mine[48:88] * EG[pl.ds(base + 30, 1), :]
                 other = jnp.concatenate([other, jnp.zeros((8, C), F32)], 0)
                 GR[2 * chunk + q // 8 + 1, 48:CHP, (q % 8) * C : (q % 8 + 1) * C] = other.astype(BF16)
-
-        @pl.when(i == 0)
-        def _():
+                packed = jnp.where(
+                    half == r, pltpu.roll(EG[pl.ds(base, ROW), :], 2 * r + 1, 1), packed
+                )
+        ED[...] = packed
+
+        if i == 1:
             pl.semaphore_wait(barrier, n_lon + n_lat)
-            to_east.start()
-            to_west.start()
 
             @pl.when(jnp.logical_not(top))
             def _():
@@ -241,8 +199,6 @@
 
                 FB[lon] = FS[...]
 
-        @pl.when(i == 1)
-        def _():
             @pl.when(jnp.logical_not(bottom))
             def _():
                 to_south.start()
@@ -250,38 +206,19 @@
 
         return 0
 
-    lax.fori_loop(0, n16, errors_chunk, 0)
+    for i in range(n16):
+        errors_chunk(i, 0)
+    to_east.start()
+    to_west.start()
 
     @pl.when(jnp.logical_not(bottom))
     def _():
         to_north.wait_recv()
         to_nw.wait_recv()
 
-    to_east.wait_recv()
-    to_west.wait_recv()
-
-    wide = (24, C)
-    lane = lanes(wide)
-    even = (lane & 1) == 0
-
     def roll(x, by):
         return pltpu.roll(x, by, 1)
 
-    he = roll(HE[...], C - 1)
-    hw = roll(HW[...], 1)
-    ed = ED[...]
-    flux_e = he[32:56] * he[26:27]
-    across_e = he[32:56] * he[27:28]
-    corner = CSE[8:32, :] * CSE[3:4, :]
-    before = jnp.where(lane == 0, corner, roll(across_e, 2))
-    tension_e = he[29:30] * (he[0:24] * he[25:26] - ed[0:24] * ed[25:26] - across_e + before)
-    across_w = hw[0:24] * hw[25:26]
-    summed_w = hw[28:29] * (ed[32:56] * ed[26:27] - hw[32:56] * hw[26:27])
-    edge_a = jnp.where(even, flux_e, across_w)
-    edge_b = jnp.where(even, tension_e, summed_w)
-
-    lane8 = lanes((8, C))
-
     def u_at(base, g):
         return EG[pl.ds(base + 8 * g, 8), :]
 
@@ -291,43 +228,43 @@
     def coef(base, k):
         return EG[pl.ds(base + 24 + k, 1), :]
 
-    def shifted_west(x, edge):
-        return jnp.where(lane8 == 0, edge, roll(x, 1))
-
-    def shifted_east(x, edge):
-        return jnp.where(lane8 == C - 1, edge, roll(x, C - 1))
+    def west_of(x):
+        return roll(x, 1)
+
+    def east_of(x):
+        return roll(x, C - 1)
 
     first = []
     for g in range(3):
         uf0 = u_at(ROW, g) * coef(ROW, 0)
         va0 = v_at(ROW, g) * coef(ROW, 3)
-        ra0 = roll(edge_a[8 * g : 8 * g + 8], C - 1)
         ua0 = u_at(ROW, g) * coef(ROW, 1)
         before = v_at(0, g) * coef(0, 3)
-        ct0 = coef(ROW, 5) * (ua0 - shifted_west(ua0, ra0) - va0 + before)
+        ct0 = coef(ROW, 5) * (ua0 - west_of(ua0) - va0 + before)
         df0 = coef(0, 7) * (u_at(0, g) * coef(0, 0) - uf0)
-        first.append((uf0, va0, ct0, df0, ra0))
+        first.append((uf0, va0, ct0, df0))
 
     ACC[...] = jnp.zeros_like(ACC)
-    CW[...] = jnp.zeros_like(CW)
 
     GR[0] = jnp.zeros(GR.shape[1:], BF16)
 
     def weight_chunk(slot, chunk):
-        cells = F[pl.ds(pl.multiple_of(8 * chunk, 8), 8), :, :].reshape(8 * C, ft)
+        cells = F[8 * chunk : 8 * chunk + 8, :, :].reshape(8 * C, ft)
         ACC[...] += jnp.dot(GR[slot], cells, preferred_element_type=F32)
+        rows = slice(8 * chunk, 8 * chunk + 8)
+        sides = [F[rows, 0:16, :].reshape(128, ft), F[rows, C - 16 : C, :].reshape(128, ft)]
+        FE[16 * chunk : 16 * chunk + 16, :] = jnp.dot(
+            choose, jnp.concatenate(sides, 0), preferred_element_type=F32
+        ).astype(BF16)
 
     def stencil_chunk(i, carry):
         last = i == n8 - 1
 
-        @pl.when(last)
-        def _():
+        if last:
             @pl.when(jnp.logical_not(top))
             def _():
                 to_south.wait_recv()
                 to_se.wait_recv()
-
-            CW[...] = roll(CNW[0:24, :] * CNW[25:26, :], 1)
 
             @pl.when(top)
             def _():
@@ -336,54 +273,93 @@
                     slot = lax.rem(lon + n_lon - d, n_lon)
                     fold_copy(slot, d, slot).wait_recv()
 
+                wide = (24, C)
                 mirror = Pv[pl.ds(lon, 1), :]
                 which = jnp.broadcast_to(mirror >> 7, wide)
                 within = jnp.broadcast_to(mirror & 127, wide)
 
-                def look(b, found):
+                found = jnp.zeros(wide, F32)
+                for b in range(n_lon):
                     there = jnp.take_along_axis(FB[b], within, axis=1, mode="promise_in_bounds")
-                    return jnp.where(which == b, there, found)
-
-                found = lax.fori_loop(0, n_lon, look, jnp.zeros(wide, F32))
+                    found = jnp.where(which == b, there, found)
                 beyond = (R + 1) * ROW
                 EG[beyond : beyond + 24, :] = -found
                 EG[beyond + 24 : beyond + 25, :] = jnp.ones((1, C), F32)
                 at = R * ROW + 31
                 EG[at : at + 1, :] = EG[at : at + 1, :] + found[23:24]
 
-        weight_chunk(i, jnp.maximum(i - 1, 0))
+        weight_chunk(i, max(i - 1, 0))
         after = []
         for g in range(3):
-            uf, va, ct, df, ra = carry[g]
-            mine_a = edge_a[8 * g : 8 * g + 8]
-            mine_b = edge_b[8 * g : 8 * g + 8]
+            uf, va, ct, df = carry[g]
             for j in range(8):
                 r = 8 * i + j
-                b0 = pl.multiple_of((r + 1) * ROW, 8)
-                b1 = pl.multiple_of((r + 2) * ROW, 8)
+                b0 = (r + 1) * ROW
+                b1 = (r + 2) * ROW
                 u1, v1 = u_at(b1, g), v_at(b1, g)
                 uf1, ua1, va1 = u1 * coef(b1, 0), u1 * coef(b1, 1), v1 * coef(b1, 3)
-                ra1 = roll(mine_a, lax.rem(4 * C - 3 - 2 * r, C))
-                if j == 7:
-                    ra1 = jnp.where(last, CW[8 * g : 8 * g + 8, :], ra1)
-                rb = roll(mine_b, C - 1 - 2 * r)
                 df1 = coef(b0, 7) * (uf - uf1)
-                ct1 = coef(b1, 5) * (ua1 - shifted_west(ua1, ra1) - va1 + va)
+                ct1 = coef(b1, 5) * (ua1 - west_of(ua1) - va1 + va)
                 vf = v_at(b0, g) * coef(b0, 2)
-                summed = coef(b0, 4) * (shifted_east(vf, ra) - vf)
-                grad_v = shifted_west(summed, rb) - summed
-                grad_uy = ct - shifted_east(ct, rb)
+                summed = coef(b0, 4) * (east_of(vf) - vf)
+                grad_v = west_of(summed) - summed
+                grad_uy = ct - east_of(ct)
                 gu = coef(b0, 0) * (df1 - df) + coef(b0, 1) * grad_uy
                 gv = coef(b0, 2) * grad_v + coef(b0, 3) * (ct1 - ct)
                 GR[i + 1, 16 * g : 16 * g + 16, j * C : (j + 1) * C] = jnp.concatenate(
                     [gu, gv], 0
                 ).astype(BF16)
-                uf, va, ct, df, ra = uf1, va1, ct1, df1, ra1
-            after.append((uf, va, ct, df, ra))
+                uf, va, ct, df = uf1, va1, ct1, df1
+            after.append((uf, va, ct, df))
         return tuple(after)
 
-    lax.fori_loop(0, n8, stencil_chunk, tuple(first))
+    carry = tuple(first)
+    for i in range(n8):
+        carry = stencil_chunk(i, carry)
     weight_chunk(n8, n8 - 1)
+
+    to_east.wait_recv()
+    to_west.wait_recv()
+    lane = lanes((24, C))
+    even = (lane & 1) == 0
+    ends = lane >= 2 * R - 2
+    ed = ED[...]
+    swap = jnp.where((lanes((ROW, C)) & 1) == 0, roll(ed, C - 1), roll(ed, 1))
+    beside = jnp.where((lanes((ROW, C)) & 1) == 0, roll(HE[...], C - 1), roll(HW[...], 1))
+
+    def part(x, k):
+        return x[24 + k : 25 + k]
+
+    u_own, v_own = ed[0:24], ed[32:56]
+    u_swap, v_swap = swap[0:24], swap[32:56]
+    u_side, v_side = beside[0:24], beside[32:56]
+    ua_own, ua_swap, ua_side = u_own * part(ed, 1), u_swap * part(swap, 1), u_side * part(beside, 1)
+    vf_own, vf_swap, vf_side = v_own * part(ed, 2), v_swap * part(swap, 2), v_side * part(beside, 2)
+    va_swap, va_side = v_swap * part(swap, 3), v_side * part(beside, 3)
+    corner = CSE[8:32, :] * CSE[3:4, :]
+    below = EG[32:56, :] * EG[27:28, :]
+    va_side0 = jnp.where(lane == 0, corner, roll(va_side, 2))
+    va_swap0 = jnp.where(lane == 0, below, roll(va_swap, 2))
+    ct_side = part(beside, 5) * (ua_side - ua_own - va_side + va_side0)
+    ct_swap = part(swap, 5) * (ua_swap - ua_own - va_swap + va_swap0)
+    gap = part(ed, 5) * (ua_swap - ua_side)
+    beyond = (R + 1) * ROW
+    ua_up = EG[beyond : beyond + 24, :] * EG[beyond + 25 : beyond + 26, :]
+    ua_far = CNW[0:24, :] * CNW[25:26, :]
+    hw_up = jnp.broadcast_to(EG[beyond + 29 : beyond + 30, :], (24, C))
+    gap_up = hw_up * roll(ua_up - ua_far, 1)
+    gap_up = jnp.where(ends, roll(gap_up, 2 * R - 1), roll(gap, C - 2))
+    fix_u = part(ed, 1) * jnp.where(even, ct_swap - ct_side, gap)
+    flux_e = part(ed, 4) * (vf_swap - vf_side)
+    flux_w = part(beside, 4) * (vf_own - vf_side) - part(swap, 4) * (vf_own - vf_swap)
+    fix_v = part(ed, 2) * jnp.where(even, flux_e, flux_w)
+    fix_v = fix_v + jnp.where(even, 0.0, part(ed, 3) * (gap_up - gap))
+    fix = []
+    for g in range(3):
+        fix += [fix_u[8 * g : 8 * g + 8], fix_v[8 * g : 8 * g + 8]]
+    fix = jnp.concatenate(fix, 0)
+    DX[...] = fix
+    ACC[0:48, :] += jnp.dot(fix[:, 0 : 2 * R].astype(BF16), FE[...], preferred_element_type=F32)
 
     scale = 1.0 / (R * n_lat * C * n_lon)
     acc = ACC[...] * scale
@@ -403,6 +379,13 @@
 
     @pl.loop(0, n8)
     def _(i):
+        at_ends = lanes((48, C))
+        at_ends = (at_ends == 0) | (at_ends == C - 1)
+        for j in range(8):
+            here = (i + 1, slice(0, 48), slice(j * C, (j + 1) * C))
+            held = GR[here].astype(F32)
+            more = roll(DX[...], C - 1 - 2 * (8 * i + j))
+            GR[here] = jnp.where(at_ends, held + more, held).astype(BF16)
         pltpu.make_async_copy(GR.at[i + 1], gr_out.at[i], gsem.at[i]).start()
 
     RB[lon] = WS[pl.ds(pl.multiple_of(lon * blk, blk), blk), :]
@@ -423,19 +406,33 @@
             device_id=(lon, lax.rem(lat + d, n_lat)), device_id_type=MESH,
         )
 
+    def when_upper(d):
+        return pl.when(lax.rem(lat + d, n_lat) >= n_lat // 2)
+
     for d in range(1, n_lat):
-        lat_copy(d).start()
+
+        @when_upper(d)
+        def _(d=d):
+            lat_copy(d).start()
+
+    wg_out[...] = jnp.zeros_like(wg_out)
+
+    @when_upper(0)
+    def _():
+        for d in range(1, n_lat):
+            lat_copy(d).wait_recv()
+        total = LB[0]
+        for k in range(1, n_lat):
+            total = total + LB[k]
+        pieces = [total[:, 16 * g : 16 * g + 8] for g in range(2)] + [total[:, 32:35]]
+        pieces += [total[:, 16 * g + 8 : 16 * g + 16] for g in range(2)] + [total[:, 40:43]]
+        wg_out[...] = jnp.concatenate(pieces + [total[:, 48:86]], 1)
+
     for d in range(1, n_lat):
-        lat_copy(d).wait_recv()
-    total = LB[0]
-    for k in range(1, n_lat):
-        total = total + LB[k]
-    pieces = [total[:, 16 * g : 16 * g + 8] for g in range(2)] + [total[:, 32:35]]
-    pieces += [total[:, 16 * g + 8 : 16 * g + 16] for g in range(2)] + [total[:, 40:43]]
-    wg_out[...] = jnp.concatenate(pieces + [total[:, 48:86]], 1)
-
-    for d in range(1, n_lat):
-        lat_copy(d).wait_send()
+
+        @when_upper(d)
+        def _(d=d):
+            lat_copy(d).wait_send()
 
     @pl.loop(1, n_lon)
     def _(d):
@@ -505,8 +502,8 @@
         out_specs=(hbm, hbm, vmem),
         scratch_shapes=[
             V((R, C, ft), BF16),
-            V((ch, R, C), BF16),
-            V(((ch + 4) * R, C), F32),
+            V((ch + 4, R, C), BF16),
+            V((R, 88, C), F32),
             V((6, R, C), F32),
             V((4, R, C), jnp.int32),
             V((ch, ft), BF16),
@@ -515,11 +512,11 @@
             V(((R + 2) * ROW, C), F32),
             V((ROW, C), F32),
             V((2 * R, ft), BF16),
+            V((48, C), F32),
             V((ROW, C), F32),
             V((ROW, C), F32),
             V((32, C), F32),
             V((32, C), F32),
-            V((24, C), F32),
             V((24, C), F32),
             V((n_lon, 24, C), F32),
             V((n8 + 1, CHP, 8 * C), BF16),
@@ -527,7 +524,7 @@
             V((ft, C), F32),
             V((n_lon, blk, C), F32),
             V((n_lat, blk, C), F32),
-            D((R // 16,)), D((2,)), D((6,)), D((n8,)), D((6,)), D((6,)),
+            D((R // 16,)), D((6,)), D((n8,)), D((6,)), D((6,)),
             D((n_lon,)), D((n_lon,)), D((n_lon,)), D((n_lon,)), D((n_lat,)), D((n_lat,)),
         ],
         compiler_params=pltpu.CompilerParams(
@@ -558,7 +555,9 @@
         ),
         name="feature_grad",
     )(gr, wp)
-    return feature_grad.reshape(R, C, ft), wg
+    down = [(k, k - n_lat // 2) for k in range(n_lat // 2, n_lat)]
+    weight_grad = wg + lax.ppermute(wg, "lat", down)
+    return feature_grad.reshape(R, C, ft), weight_grad
 
 
 def solution(mesh):

time: 38.6 us -> 33.8 us (0.88)
  Pallas kernels: 37.3 us -> 30.1 us
  starting transfers between devices: 0 us -> 1.29 us
  waiting for transfers between devices: 0 us -> 1.03 us
  other arithmetic: 0 us -> 0.6 us
  local copies, waits for them, and re-layouts: 0.6 us -> 0 us
    pallas_call x1, Pallas kernels: 33.5 us -> 26.3 us  [per_device(): pl.pallas_call(grads_kernel, out_shape=(jax.ShapeDtypeStruct((n8, CHP, 8...]
    ppermute x0 -> x1, starting transfers between devices: none -> 1.29 us  [per_device(): weight_grad = wg + lax.ppermute(wg, 'lat', down)]
    ppermute x0 -> x1, waiting for transfers between devices: none -> 1.03 us  [per_device(): weight_grad = wg + lax.ppermute(wg, 'lat', down)]
    add x0 -> x1, other arithmetic: none -> 0.6 us  [per_device(): weight_grad = wg + lax.ppermute(wg, 'lat', down)]
    unnamed x1 -> x0, local copies, waits for them, and re-layouts: 0.6 us -> none
  transfers between devices with their start and end apart: 0 -> 1, of which waited for: 0 -> 1; matrix products, arithmetic and copies ran while one was open for 0% -> 0% of each run, Pallas kernels for 0% -> 11%
where the time goes in v3:
time: 33.8 us; the launch traced here: 33.7 us
  Pallas kernels  30.1 us (89%)
  starting transfers between devices  1.29 us (4%)
  waiting for transfers between devices  1.03 us (3%)
  between operations  0.66 us (2%)
  other arithmetic  0.6 us (2%)
    pallas_call x1, Pallas kernels, per_device(): pl.pallas_call(grads_kernel, out_shape=(jax.ShapeDtypeStruct((n8, CHP, 8...  26.3 us
    pallas_call x1, Pallas kernels, per_device(): pl.pallas_call(feature_kernel, out_shape=jax.ShapeDtypeStruct((cells, ft)...  3.74 us
    ppermute x1, starting transfers between devices, per_device(): weight_grad = wg + lax.ppermute(wg, 'lat', down)  1.29 us
    ppermute x1, waiting for transfers between devices, per_device(): weight_grad = wg + lax.ppermute(wg, 'lat', down)  1.03 us
  transfers between devices with their start and end apart: 1, of which 1 were waited for; matrix products, arithmetic and copies ran while one was open for 0% of the time, Pallas kernels for 11%

profile of v3, /device:TPU:1, one launch (start us, length us, event | category | flops | bytes accessed | tf_op | source)
XLA Modules:
  0.0 33.7 jit_solution(296408327427344359)
XLA Ops:
  0.6 26.3 %grads_and_weight_grad.1 = (bf16[8,96,1024]{2,1,0:T(8,128)(2,1)S(1)}, bf16[96,512]{1,0:T(8,128)(2,1)S(1)}, f32[16,76]{1,0:T(8,128)S(1)}) custom-call(bf16[64,128,512]{2,1,0:T(8,128)(2,1)} %feat.1, bf16[76,64,128]{2,1,0:T(8,128)(2,1)} %tgt.1, f32[6,64,128]{2,1,0:T(8,128)} %met.1, s32[4,64,128]{2,1,0:T(8,128)} %msk.1, bf16[76,512]{1,0:T(8,128)(2,1)} %bitcast.4, ...), custom_call_target="tpu_custom_call" | custom-call | flops 1610612736 | bytes 12582912 | tf_op jit(solution)/shard_map/grads_and_weight_grad/pallas_call | solution.py:494
  27.0 1.3 %collective-permute-start = (f32[16,76]{1,0:T(8,128)S(1)}, f32[16,76]{1,0:T(8,128)S(1)}, u32[]{:S(2)}, u32[]{:S(2)}) collective-permute-start(f32[16,76]{1,0:T(8,128)S(1)} %get-tuple-element.7), channel_id=1, source_target_pairs={{2,0},{3,1},{6,4},{7,5},{10,8},{11,9},{14,12},{15,13},{18,16},{19,... | collective-permute-start | bytes 14600 | tf_op jit(solution)/shard_map/ppermute | solution.py:559
  28.3 3.7 %feature_grad.1 = bf16[8192,512]{1,0:T(8,128)(2,1)} custom-call(bf16[8,96,1024]{2,1,0:T(8,128)(2,1)S(1)} %get-tuple-element.5.gr, bf16[96,512]{1,0:T(8,128)(2,1)S(1)} %get-tuple-element.6.wp), custom_call_target="tpu_custom_call" | custom-call | flops 805306368 | bytes 10485760 | tf_op jit(solution)/shard_map/feature_grad/pallas_call | solution.py:546
  32.0 1.0 %collective-permute-done = f32[16,76]{1,0:T(8,128)S(1)} collective-permute-done((f32[16,76]{1,0:T(8,128)S(1)}, f32[16,76]{1,0:T(8,128)S(1)}, u32[]{:S(2)}, u32[]{:S(2)}) %collective-permute-start) | collective-permute-done | bytes 4896 | tf_op jit(solution)/shard_map/ppermute | solution.py:559
  33.1 0.6 %add.3 = f32[16,76]{1,0:T(8,128)} add(f32[16,76]{1,0:T(8,128)S(1)} %get-tuple-element.7, f32[16,76]{1,0:T(8,128)S(1)} %collective-permute-done) | non-fusion elementwise | flops 1216 | bytes 14592 | tf_op jit(solution)/shard_map/add | solution.py:559
Async XLA Ops:
  27.0 6.1 %collective-permute-start = (f32[16,76]{1,0:T(8,128)S(1)}, f32[16,76]{1,0:T(8,128)S(1)}, u32[]{:S(2)}, u32[]{:S(2)}) collective-permute-start(f32[16,76]{1,0:T(8,128)S(1)} %get-tuple-element.7), channel_id=1, source_target_pairs={{2,0},{3,1},{6,4},{7,5},{10,8},{11,9},{14,12},{15,13},{18,16},{19,... | collective-permute-start | bytes 14600 | tf_op jit(solution)/shard_map/ppermute | solution.py:559

commit v4 on v3

--- a/solution.py
+++ b/solution.py
@@ -23,8 +23,8 @@
 
 def grads_kernel(
     feat, tgt, met, msk, wt, part, gr_out, wp_out, wg_out,
-    F, Tb, Tf, M, K, Wv, Pv, Wp, EG, ED, FE, DX, HW, HE, CNW, CSE, FS, FB, GR, ACC, WS, RB, LB,
-    fsem, lsem, gsem, hs, hr, fs_s, fs_r, rs_s, rs_r, ls_s, ls_r,
+    F, FR, RS, Tb, Tf, M, K, Wv, Pv, Wp, EG, ED, FE, FT, DX, HW, HE, CNW, CSE, FS, FB, GR, ACC, WS, RB, LB,
+    fsem, esem, lsem, gsem, hs, hr, fs_s, fs_r, rs_s, rs_r, ls_s, ls_r,
 ):
     n_lon, n_lat = lax.axis_size("lon"), lax.axis_size("lat")
     lon, lat = lax.axis_index("lon"), lax.axis_index("lat")
@@ -50,9 +50,17 @@
     pl.semaphore_signal(barrier, inc=1, device_id=(west, up), device_id_type=MESH)
 
     def fcopy(c):
-        at = pl.ds(c * 16, 16)
+        at = (pl.ds(c * 16, 16), pl.ds(16, C - 32))
         return pltpu.make_async_copy(feat.at[at], F.at[at], fsem.at[c])
 
+    def ecopy(k):
+        at = (pl.ds(0, R), pl.ds(k * (C - 16), 16))
+        return pltpu.make_async_copy(feat.at[at], F.at[at], esem.at[k])
+
+    rows_in = [
+        pltpu.make_async_copy(feat.at[0:1], FR.at[0:1], esem.at[2]),
+        pltpu.make_async_copy(feat.at[R - 1 : R], FR.at[1:2], esem.at[3]),
+    ]
     small = [
         pltpu.make_async_copy(met, M, lsem.at[0]),
         pltpu.make_async_copy(msk, K, lsem.at[1]),
@@ -62,6 +70,10 @@
     ]
     for copy in small:
         copy.start()
+    for copy in rows_in:
+        copy.start()
+    ecopy(0).start()
+    ecopy(1).start()
     for i in range(n16):
         fcopy((i + n16 - 1) % n16).start()
 
@@ -123,11 +135,53 @@
 
     lax.fori_loop(0, n16, widen, 0)
 
-    q = lax.broadcasted_iota(jnp.int32, (16, 256), 0)
-    cell = lax.broadcasted_iota(jnp.int32, (16, 256), 1)
-    wanted = (q >> 1) * 16 + jnp.where((q & 1) == 1, 0, 128 + 15)
+    half8 = lanes((8, C)) >> 1
+
+    def pack(i, packed):
+        packed = list(packed)
+        for j in range(16):
+            r = 16 * i + j
+            base = pl.multiple_of((r + 1) * ROW, 8)
+            rows = [Tf[r, 8 * k : 8 * k + 8, :] for k in range(6)]
+            rows.append(EG[pl.ds(base + 24, 8), :])
+            by = 2 * r + 1
+            packed = [
+                jnp.where(half8 == r, pltpu.roll(x, by, 1), y) for x, y in zip(rows, packed)
+            ]
+        return tuple(packed)
+
+    packed = lax.fori_loop(0, n16, pack, (jnp.zeros((8, C), F32),) * 7)
+    for copy in rows_in:
+        copy.wait()
+    at_rows = lax.dot_general(
+        Wp[0:48, :], FR[...].reshape(2 * C, ft), NT, preferred_element_type=F32
+    )
+    for k, r in enumerate((0, R - 1)):
+        found = at_rows[:, k * C : (k + 1) * C] - Tf[r, 0:48, :]
+        to = k * ROW
+        for g in range(3):
+            RS[to + 8 * g : to + 8 * g + 8, :] = found[16 * g : 16 * g + 8]
+            RS[to + 32 + 8 * g : to + 40 + 8 * g, :] = found[16 * g + 8 : 16 * g + 16]
+        RS[to + 24 : to + 32, :] = EG[(r + 1) * ROW + 24 : (r + 1) * ROW + 32, :]
+
+    q = lax.broadcasted_iota(jnp.int32, (32, 512), 0)
+    cell = lax.broadcasted_iota(jnp.int32, (32, 512), 1)
+    wanted = (q >> 1) * 16 + jnp.where((q & 1) == 1, 0, 256 + 15)
     choose = jnp.where(cell == wanted, 1.0, 0.0).astype(BF16)
+    ecopy(0).wait()
+    ecopy(1).wait()
+    for i in range(n16):
+        rows = slice(16 * i, 16 * i + 16)
+        sides = [F[rows, 0:16, :].reshape(256, ft), F[rows, C - 16 : C, :].reshape(256, ft)]
+        FE[32 * i : 32 * i + 32, :] = jnp.dot(
+            choose, jnp.concatenate(sides, 0), preferred_element_type=F32
+        ).astype(BF16)
+    at_edges = lax.dot_general(Wp[0:48, :], FE[...], NT, preferred_element_type=F32)
     ED[...] = jnp.zeros_like(ED)
+    for k in range(6):
+        to = 8 * (k // 2) + 32 * (k % 2)
+        ED[to : to + 8, 0 : 2 * R] = at_edges[8 * k : 8 * k + 8] - packed[k][:, 0 : 2 * R]
+    ED[24:32, :] = packed[6]
 
     def send(src, dst, k, device):
         return pltpu.make_async_remote_copy(
@@ -136,29 +190,59 @@
         )
 
     south_row = EG.at[0:ROW]
-    first_row = EG.at[ROW : 2 * ROW]
-    last_row = EG.at[R * ROW : (R + 1) * ROW]
+    first_row = RS.at[0:ROW]
+    last_row = RS.at[ROW : 2 * ROW]
     north_row = EG.at[(R + 1) * ROW : (R + 2) * ROW]
     to_north = send(last_row, south_row, 0, (lon, up))
     to_south = send(first_row, north_row, 1, (lon, down))
     to_east = send(ED, HW, 2, (east, lat))
     to_west = send(ED, HE, 3, (west, lat))
-    to_nw = send(EG.at[R * ROW + 24 : (R + 1) * ROW], CSE, 4, (west, up))
-    to_se = send(EG.at[ROW : ROW + 32], CNW, 5, (east, down))
-
-    def fold_copy(peer, d, slot):
+    to_nw = send(RS.at[ROW + 24 : 2 * ROW], CSE, 4, (west, up))
+    to_se = send(RS.at[0:32], CNW, 5, (east, down))
+
+    def fold_copy(peer):
         return pltpu.make_async_remote_copy(
-            src_ref=FS, dst_ref=FB.at[slot], send_sem=fs_s.at[d], recv_sem=fs_r.at[slot],
-            device_id=(peer, lat), device_id_type=MESH,
-        )
-
-    half = lanes((ROW, C)) >> 1
+            src_ref=FS, dst_ref=FB.at[pl.ds(pl.multiple_of(lon * 24, 8), 24)],
+            send_sem=fs_s, recv_sem=fs_r, device_id=(peer, lat), device_id_type=MESH,
+        )
+
+    others = pl.ds(0, (n_lon - 1) * 24)
+    fold_all = pltpu.make_async_remote_copy(
+        src_ref=FB.at[others], dst_ref=FB.at[others], send_sem=fs_s, recv_sem=fs_r,
+        device_id=(east, lat), device_id_type=MESH,
+    )
+
+    pl.semaphore_wait(barrier, n_lon + n_lat)
+
+    @pl.when(jnp.logical_not(top))
+    def _():
+        to_nw.start()
+        to_north.start()
+
+    @pl.when(jnp.logical_not(bottom))
+    def _():
+        to_se.start()
+        to_south.start()
+
+    to_east.start()
+    to_west.start()
+
+    @pl.when(top)
+    def _():
+        flux = RS[ROW : ROW + 24, :] * RS[ROW + 24 : ROW + 25, :]
+        sub = lax.broadcasted_iota(jnp.int32, (24, C), 0)
+        FS[...] = jnp.where(sub == 23, RS[ROW + 28 : ROW + 29, :], flux)
+
+        @pl.loop(1, n_lon)
+        def _(d):
+            fold_copy(lax.rem(lon + d, n_lon)).start()
+
+        FB[pl.ds(pl.multiple_of(lon * 24, 8), 24), :] = FS[...]
 
     def errors_chunk(i, _):
         chunk = (i + n16 - 1) % n16
         r0 = chunk * 16
         fcopy(chunk).wait()
-        packed = ED[...]
         for j4 in range(4):
             cells = F[pl.ds(r0 + 4 * j4, 4), :, :].reshape(4 * C, ft)
             predicted = lax.dot_general(Wp[...], cells, NT, preferred_element_type=F32)
@@ -173,48 +257,11 @@
                 other = mine[48:88] * EG[pl.ds(base + 30, 1), :]
                 other = jnp.concatenate([other, jnp.zeros((8, C), F32)], 0)
                 GR[2 * chunk + q // 8 + 1, 48:CHP, (q % 8) * C : (q % 8 + 1) * C] = other.astype(BF16)
-                packed = jnp.where(
-                    half == r, pltpu.roll(EG[pl.ds(base, ROW), :], 2 * r + 1, 1), packed
-                )
-        ED[...] = packed
-
-        if i == 1:
-            pl.semaphore_wait(barrier, n_lon + n_lat)
-
-            @pl.when(jnp.logical_not(top))
-            def _():
-                to_north.start()
-                to_nw.start()
-
-            @pl.when(top)
-            def _():
-                row = R * ROW
-                flux = EG[row : row + 24, :] * EG[row + 24 : row + 25, :]
-                sub = lax.broadcasted_iota(jnp.int32, (24, C), 0)
-                FS[...] = jnp.where(sub == 23, EG[row + 28 : row + 29, :], flux)
-
-                @pl.loop(1, n_lon)
-                def _(d):
-                    fold_copy(lax.rem(lon + d, n_lon), d, lon).start()
-
-                FB[lon] = FS[...]
-
-            @pl.when(jnp.logical_not(bottom))
-            def _():
-                to_south.start()
-                to_se.start()
 
         return 0
 
     for i in range(n16):
         errors_chunk(i, 0)
-    to_east.start()
-    to_west.start()
-
-    @pl.when(jnp.logical_not(bottom))
-    def _():
-        to_north.wait_recv()
-        to_nw.wait_recv()
 
     def roll(x, by):
         return pltpu.roll(x, by, 1)
@@ -234,44 +281,37 @@
     def east_of(x):
         return roll(x, C - 1)
 
-    first = []
-    for g in range(3):
-        uf0 = u_at(ROW, g) * coef(ROW, 0)
-        va0 = v_at(ROW, g) * coef(ROW, 3)
-        ua0 = u_at(ROW, g) * coef(ROW, 1)
-        before = v_at(0, g) * coef(0, 3)
-        ct0 = coef(ROW, 5) * (ua0 - west_of(ua0) - va0 + before)
-        df0 = coef(0, 7) * (u_at(0, g) * coef(0, 0) - uf0)
-        first.append((uf0, va0, ct0, df0))
+    def state_at(r):
+        b0, b1 = r * ROW, (r + 1) * ROW
+        state = []
+        for g in range(3):
+            uf = u_at(b1, g) * coef(b1, 0)
+            va = v_at(b1, g) * coef(b1, 3)
+            ua = u_at(b1, g) * coef(b1, 1)
+            before = v_at(b0, g) * coef(b0, 3)
+            ct = coef(b1, 5) * (ua - west_of(ua) - va + before)
+            df = coef(b0, 7) * (u_at(b0, g) * coef(b0, 0) - uf)
+            state.append((uf, va, ct, df))
+        return state
 
     ACC[...] = jnp.zeros_like(ACC)
 
-    GR[0] = jnp.zeros(GR.shape[1:], BF16)
 
     def weight_chunk(slot, chunk):
         cells = F[8 * chunk : 8 * chunk + 8, :, :].reshape(8 * C, ft)
         ACC[...] += jnp.dot(GR[slot], cells, preferred_element_type=F32)
-        rows = slice(8 * chunk, 8 * chunk + 8)
-        sides = [F[rows, 0:16, :].reshape(128, ft), F[rows, C - 16 : C, :].reshape(128, ft)]
-        FE[16 * chunk : 16 * chunk + 16, :] = jnp.dot(
-            choose, jnp.concatenate(sides, 0), preferred_element_type=F32
-        ).astype(BF16)
-
-    def stencil_chunk(i, carry):
+
+    def stencil_chunk(i, carry, done):
         last = i == n8 - 1
 
         if last:
             @pl.when(jnp.logical_not(top))
             def _():
                 to_south.wait_recv()
-                to_se.wait_recv()
 
             @pl.when(top)
             def _():
-                @pl.loop(1, n_lon)
-                def _(d):
-                    slot = lax.rem(lon + n_lon - d, n_lon)
-                    fold_copy(slot, d, slot).wait_recv()
+                fold_all.wait_recv()
 
                 wide = (24, C)
                 mirror = Pv[pl.ds(lon, 1), :]
@@ -280,7 +320,9 @@
 
                 found = jnp.zeros(wide, F32)
                 for b in range(n_lon):
-                    there = jnp.take_along_axis(FB[b], within, axis=1, mode="promise_in_bounds")
+                    there = jnp.take_along_axis(
+                        FB[24 * b : 24 * b + 24, :], within, axis=1, mode="promise_in_bounds"
+                    )
                     found = jnp.where(which == b, there, found)
                 beyond = (R + 1) * ROW
                 EG[beyond : beyond + 24, :] = -found
@@ -288,7 +330,8 @@
                 at = R * ROW + 31
                 EG[at : at + 1, :] = EG[at : at + 1, :] + found[23:24]
 
-        weight_chunk(i, max(i - 1, 0))
+        if done is not None:
+            weight_chunk(done + 1, done)
         after = []
         for g in range(3):
             uf, va, ct, df = carry[g]
@@ -313,45 +356,74 @@
             after.append((uf, va, ct, df))
         return tuple(after)
 
-    carry = tuple(first)
-    for i in range(n8):
-        carry = stencil_chunk(i, carry)
-    weight_chunk(n8, n8 - 1)
+    carry, done = state_at(8), None
+    for i in [*range(1, n8 - 1), 0, n8 - 1]:
+        if i == 0:
+            kept = carry
+
+            @pl.when(jnp.logical_not(bottom))
+            def _():
+                to_north.wait_recv()
+
+            carry = state_at(0)
+        elif i == n8 - 1:
+            carry = kept
+        carry = stencil_chunk(i, carry, done)
+        done = i
+    weight_chunk(done + 1, done)
+
+    lane = lanes((24, C))
+    even = (lane & 1) == 0
+    even_row = (lanes((ROW, C)) & 1) == 0
+    ends = lane >= 2 * R - 2
+    ed = ED[...]
+    swap = jnp.where(even_row, roll(ed, C - 1), roll(ed, 1))
+
+    def part(x, k):
+        return x[24 + k : 25 + k]
+
+    u_own, v_own = ed[0:24], ed[32:56]
+    u_swap, v_swap = swap[0:24], swap[32:56]
+    ua_own, ua_swap = u_own * part(ed, 1), u_swap * part(swap, 1)
+    vf_own, vf_swap = v_own * part(ed, 2), v_swap * part(swap, 2)
+    va_swap = v_swap * part(swap, 3)
+    below = EG[32:56, :] * EG[27:28, :]
+    ct_swap = part(swap, 5) * (ua_swap - ua_own - va_swap + jnp.where(lane == 0, below, roll(va_swap, 2)))
+    flux_swap = part(swap, 4) * (vf_own - vf_swap)
+    beyond = (R + 1) * ROW
+    ua_up = EG[beyond : beyond + 24, :] * EG[beyond + 25 : beyond + 26, :]
+    hw_up = jnp.broadcast_to(EG[beyond + 29 : beyond + 30, :], (24, C))
+
+    scale = 1.0 / (R * n_lat * C * n_lon)
+    acc = jnp.concatenate([ACC[...] * scale, jnp.zeros((C - CHP, ft), F32)], 0)
+    WS[...] = acc.T
+    FT[...] = FE[...].T
 
     to_east.wait_recv()
     to_west.wait_recv()
-    lane = lanes((24, C))
-    even = (lane & 1) == 0
-    ends = lane >= 2 * R - 2
-    ed = ED[...]
-    swap = jnp.where((lanes((ROW, C)) & 1) == 0, roll(ed, C - 1), roll(ed, 1))
-    beside = jnp.where((lanes((ROW, C)) & 1) == 0, roll(HE[...], C - 1), roll(HW[...], 1))
-
-    def part(x, k):
-        return x[24 + k : 25 + k]
-
-    u_own, v_own = ed[0:24], ed[32:56]
-    u_swap, v_swap = swap[0:24], swap[32:56]
+
+    @pl.when(jnp.logical_not(bottom))
+    def _():
+        to_nw.wait_recv()
+
+    @pl.when(jnp.logical_not(top))
+    def _():
+        to_se.wait_recv()
+
+    corner = CSE[8:32, :] * CSE[3:4, :]
+    ua_far = CNW[0:24, :] * CNW[25:26, :]
+    gap_top = roll(hw_up * roll(ua_up - ua_far, 1), 2 * R - 1)
+    beside = jnp.where(even_row, roll(HE[...], C - 1), roll(HW[...], 1))
     u_side, v_side = beside[0:24], beside[32:56]
-    ua_own, ua_swap, ua_side = u_own * part(ed, 1), u_swap * part(swap, 1), u_side * part(beside, 1)
-    vf_own, vf_swap, vf_side = v_own * part(ed, 2), v_swap * part(swap, 2), v_side * part(beside, 2)
-    va_swap, va_side = v_swap * part(swap, 3), v_side * part(beside, 3)
-    corner = CSE[8:32, :] * CSE[3:4, :]
-    below = EG[32:56, :] * EG[27:28, :]
+    ua_side, vf_side = u_side * part(beside, 1), v_side * part(beside, 2)
+    va_side = v_side * part(beside, 3)
     va_side0 = jnp.where(lane == 0, corner, roll(va_side, 2))
-    va_swap0 = jnp.where(lane == 0, below, roll(va_swap, 2))
     ct_side = part(beside, 5) * (ua_side - ua_own - va_side + va_side0)
-    ct_swap = part(swap, 5) * (ua_swap - ua_own - va_swap + va_swap0)
+    flux_e = part(ed, 4) * (vf_swap - vf_side)
     gap = part(ed, 5) * (ua_swap - ua_side)
-    beyond = (R + 1) * ROW
-    ua_up = EG[beyond : beyond + 24, :] * EG[beyond + 25 : beyond + 26, :]
-    ua_far = CNW[0:24, :] * CNW[25:26, :]
-    hw_up = jnp.broadcast_to(EG[beyond + 29 : beyond + 30, :], (24, C))
-    gap_up = hw_up * roll(ua_up - ua_far, 1)
-    gap_up = jnp.where(ends, roll(gap_up, 2 * R - 1), roll(gap, C - 2))
+    gap_up = jnp.where(ends, gap_top, roll(gap, C - 2))
+    flux_w = part(beside, 4) * (vf_own - vf_side) - flux_swap
     fix_u = part(ed, 1) * jnp.where(even, ct_swap - ct_side, gap)
-    flux_e = part(ed, 4) * (vf_swap - vf_side)
-    flux_w = part(beside, 4) * (vf_own - vf_side) - part(swap, 4) * (vf_own - vf_swap)
     fix_v = part(ed, 2) * jnp.where(even, flux_e, flux_w)
     fix_v = fix_v + jnp.where(even, 0.0, part(ed, 3) * (gap_up - gap))
     fix = []
@@ -359,23 +431,27 @@
         fix += [fix_u[8 * g : 8 * g + 8], fix_v[8 * g : 8 * g + 8]]
     fix = jnp.concatenate(fix, 0)
     DX[...] = fix
-    ACC[0:48, :] += jnp.dot(fix[:, 0 : 2 * R].astype(BF16), FE[...], preferred_element_type=F32)
-
-    scale = 1.0 / (R * n_lat * C * n_lon)
-    acc = ACC[...] * scale
-    acc = jnp.concatenate([acc, jnp.zeros((C - CHP, ft), F32)], 0)
-    WS[...] = acc.T
-
-    def rows_copy(peer, d, slot):
+    more = lax.dot_general(
+        FT[...], fix[:, 0 : 2 * R].astype(BF16), NT, preferred_element_type=F32
+    )
+    WS[:, 0:48] += more * scale
+
+    def rows_copy(peer):
         src = WS.at[pl.ds(pl.multiple_of(peer * blk, blk), blk)]
+        dst = RB.at[pl.ds(pl.multiple_of(lon * blk, blk), blk)]
         return pltpu.make_async_remote_copy(
-            src_ref=src, dst_ref=RB.at[slot], send_sem=rs_s.at[d], recv_sem=rs_r.at[slot],
+            src_ref=src, dst_ref=dst, send_sem=rs_s, recv_sem=rs_r,
             device_id=(peer, lat), device_id_type=MESH,
         )
+
+    rows_all = pltpu.make_async_remote_copy(
+        src_ref=WS.at[0 : (n_lon - 1) * blk], dst_ref=RB.at[0 : (n_lon - 1) * blk],
+        send_sem=rs_s, recv_sem=rs_r, device_id=(east, lat), device_id_type=MESH,
+    )
 
     @pl.loop(1, n_lon)
     def _(d):
-        rows_copy(lax.rem(lon + d, n_lon), d, lon).start()
+        rows_copy(lax.rem(lon + d, n_lon)).start()
 
     @pl.loop(0, n8)
     def _(i):
@@ -388,16 +464,13 @@
             GR[here] = jnp.where(at_ends, held + more, held).astype(BF16)
         pltpu.make_async_copy(GR.at[i + 1], gr_out.at[i], gsem.at[i]).start()
 
-    RB[lon] = WS[pl.ds(pl.multiple_of(lon * blk, blk), blk), :]
-
-    @pl.loop(1, n_lon)
-    def _(d):
-        slot = lax.rem(lon + n_lon - d, n_lon)
-        rows_copy(slot, d, slot).wait_recv()
-
-    total = RB[0]
+    here = pl.ds(pl.multiple_of(lon * blk, blk), blk)
+    RB[here, :] = WS[here, :]
+
+    rows_all.wait_recv()
+    total = RB[0:blk, :]
     for k in range(1, n_lon):
-        total = total + RB[k]
+        total = total + RB[k * blk : (k + 1) * blk, :]
     LB[lat] = total
 
     def lat_copy(d):
@@ -434,9 +507,7 @@
         def _(d=d):
             lat_copy(d).wait_send()
 
-    @pl.loop(1, n_lon)
-    def _(d):
-        rows_copy(lax.rem(lon + d, n_lon), d, lon).wait_send()
+    rows_all.wait_send()
 
     @pl.when(jnp.logical_not(top))
     def _():
@@ -445,9 +516,7 @@
 
     @pl.when(top)
     def _():
-        @pl.loop(1, n_lon)
-        def _(d):
-            fold_copy(lax.rem(lon + d, n_lon), d, lon).wait_send()
+        fold_all.wait_send()
 
     @pl.when(jnp.logical_not(bottom))
     def _():
@@ -502,6 +571,8 @@
         out_specs=(hbm, hbm, vmem),
         scratch_shapes=[
             V((R, C, ft), BF16),
+            V((2, C, ft), BF16),
+            V((2 * ROW, C), F32),
             V((ch + 4, R, C), BF16),
             V((R, 88, C), F32),
             V((6, R, C), F32),
@@ -512,20 +583,21 @@
             V(((R + 2) * ROW, C), F32),
             V((ROW, C), F32),
             V((2 * R, ft), BF16),
+            V((ft, 2 * R), BF16),
             V((48, C), F32),
             V((ROW, C), F32),
             V((ROW, C), F32),
             V((32, C), F32),
             V((32, C), F32),
             V((24, C), F32),
-            V((n_lon, 24, C), F32),
+            V((n_lon * 24, C), F32),
             V((n8 + 1, CHP, 8 * C), BF16),
             V((CHP, ft), F32),
             V((ft, C), F32),
-            V((n_lon, blk, C), F32),
+            V((n_lon * blk, C), F32),
             V((n_lat, blk, C), F32),
-            D((R // 16,)), D((6,)), D((n8,)), D((6,)), D((6,)),
-            D((n_lon,)), D((n_lon,)), D((n_lon,)), D((n_lon,)), D((n_lat,)), D((n_lat,)),
+            D((R // 16,)), D((4,)), D((6,)), D((n8,)), D((6,)), D((6,)),
+            D, D, D, D, D((n_lat,)), D((n_lat,)),
         ],
         compiler_params=pltpu.CompilerParams(
             collective_id=0, has_side_effects=True, vmem_limit_bytes=48 * 1024 * 1024

time: 33.8 us -> 32.3 us (0.956)
  Pallas kernels: 30.1 us -> 28.8 us
    pallas_call x1, Pallas kernels: 26.3 us -> 25.1 us  [per_device(): pl.pallas_call(grads_kernel, out_shape=(jax.ShapeDtypeStruct((n8, CHP, 8...]
  transfers between devices with their start and end apart: 1 -> 1, of which waited for: 1 -> 1; matrix products, arithmetic and copies ran while one was open for 0% -> 0% of each run, Pallas kernels for 11% -> 12%
where the time goes in v4:
time: 32.3 us; the launch traced here: 32.2 us
  Pallas kernels  28.8 us (89%)
  starting transfers between devices  1.29 us (4%)
  waiting for transfers between devices  0.85 us (3%)
  between operations  0.66 us (2%)
  other arithmetic  0.6 us (2%)
    pallas_call x1, Pallas kernels, per_device(): pl.pallas_call(grads_kernel, out_shape=(jax.ShapeDtypeStruct((n8, CHP, 8...  25.1 us
    pallas_call x1, Pallas kernels, per_device(): pl.pallas_call(feature_kernel, out_shape=jax.ShapeDtypeStruct((cells, ft)...  3.74 us
    ppermute x1, starting transfers between devices, per_device(): weight_grad = wg + lax.ppermute(wg, 'lat', down)  1.29 us
    ppermute x1, waiting for transfers between devices, per_device(): weight_grad = wg + lax.ppermute(wg, 'lat', down)  0.85 us
  transfers between devices with their start and end apart: 1, of which 1 were waited for; matrix products, arithmetic and copies ran while one was open for 0% of the time, Pallas kernels for 12%

profile of v4, /device:TPU:1, one launch (start us, length us, event | category | flops | bytes accessed | tf_op | source)
XLA Modules:
  0.0 32.2 jit_solution(10220343824055709877)
XLA Ops:
  0.6 25.1 %grads_and_weight_grad.1 = (bf16[8,96,1024]{2,1,0:T(8,128)(2,1)S(1)}, bf16[96,512]{1,0:T(8,128)(2,1)S(1)}, f32[16,76]{1,0:T(8,128)S(1)}) custom-call(bf16[64,128,512]{2,1,0:T(8,128)(2,1)} %feat.1, bf16[76,64,128]{2,1,0:T(8,128)(2,1)} %tgt.1, f32[6,64,128]{2,1,0:T(8,128)} %met.1, s32[4,64,128]{2,1,0:T(8,128)} %msk.1, bf16[76,512]{1,0:T(8,128)(2,1)} %bitcast.4, ...), custom_call_target="tpu_custom_call" | custom-call | flops 1610612736 | bytes 12582912 | tf_op jit(solution)/shard_map/grads_and_weight_grad/pallas_call | solution.py:563
  25.7 1.3 %collective-permute-start = (f32[16,76]{1,0:T(8,128)S(1)}, f32[16,76]{1,0:T(8,128)S(1)}, u32[]{:S(2)}, u32[]{:S(2)}) collective-permute-start(f32[16,76]{1,0:T(8,128)S(1)} %get-tuple-element.7), channel_id=1, source_target_pairs={{2,0},{3,1},{6,4},{7,5},{10,8},{11,9},{14,12},{15,13},{18,16},{19,... | collective-permute-start | bytes 14600 | tf_op jit(solution)/shard_map/ppermute | solution.py:631
  27.0 3.7 %feature_grad.1 = bf16[8192,512]{1,0:T(8,128)(2,1)} custom-call(bf16[8,96,1024]{2,1,0:T(8,128)(2,1)S(1)} %get-tuple-element.5.gr, bf16[96,512]{1,0:T(8,128)(2,1)S(1)} %get-tuple-element.6.wp), custom_call_target="tpu_custom_call" | custom-call | flops 805306368 | bytes 10485760 | tf_op jit(solution)/shard_map/feature_grad/pallas_call | solution.py:618
  30.8 0.9 %collective-permute-done = f32[16,76]{1,0:T(8,128)S(1)} collective-permute-done((f32[16,76]{1,0:T(8,128)S(1)}, f32[16,76]{1,0:T(8,128)S(1)}, u32[]{:S(2)}, u32[]{:S(2)}) %collective-permute-start) | collective-permute-done | bytes 4896 | tf_op jit(solution)/shard_map/ppermute | solution.py:631
  31.6 0.6 %add.3 = f32[16,76]{1,0:T(8,128)} add(f32[16,76]{1,0:T(8,128)S(1)} %get-tuple-element.7, f32[16,76]{1,0:T(8,128)S(1)} %collective-permute-done) | non-fusion elementwise | flops 1216 | bytes 14592 | tf_op jit(solution)/shard_map/add | solution.py:631
Async XLA Ops:
  25.7 5.9 %collective-permute-start = (f32[16,76]{1,0:T(8,128)S(1)}, f32[16,76]{1,0:T(8,128)S(1)}, u32[]{:S(2)}, u32[]{:S(2)}) collective-permute-start(f32[16,76]{1,0:T(8,128)S(1)} %get-tuple-element.7), channel_id=1, source_target_pairs={{2,0},{3,1},{6,4},{7,5},{10,8},{11,9},{14,12},{15,13},{18,16},{19,... | collective-permute-start | bytes 14600 | tf_op jit(solution)/shard_map/ppermute | solution.py:631

commit v5 on v4

--- a/solution.py
+++ b/solution.py
@@ -70,6 +70,12 @@
     ]
     for copy in small:
         copy.start()
+    @pl.loop(2, n_lon - 1)
+    def _(d):
+        pl.semaphore_signal(
+            barrier, inc=1, device_id=(lax.rem(lon + d, n_lon), lat), device_id_type=MESH
+        )
+
     for copy in rows_in:
         copy.start()
     ecopy(0).start()
@@ -86,12 +92,6 @@
     def _():
         EG[(R + 1) * ROW : (R + 2) * ROW, :] = jnp.zeros((ROW, C), F32)
         CNW[...] = jnp.zeros_like(CNW)
-
-    @pl.loop(2, n_lon - 1)
-    def _(d):
-        pl.semaphore_signal(
-            barrier, inc=1, device_id=(lax.rem(lon + d, n_lon), lat), device_id_type=MESH
-        )
 
     small[0].wait()
     small[1].wait()

time: 32.3 us -> 29.9 us (0.926)
  Pallas kernels: 28.8 us -> 26.4 us
    pallas_call x1, Pallas kernels: 25.1 us -> 22.6 us  [per_device(): pl.pallas_call(grads_kernel, out_shape=(jax.ShapeDtypeStruct((n8, CHP, 8...]
  transfers between devices with their start and end apart: 1 -> 1, of which waited for: 1 -> 1; matrix products, arithmetic and copies ran while one was open for 0% -> 0% of each run, Pallas kernels for 12% -> 13%
where the time goes in v5:
time: 29.9 us; the launch traced here: 29.8 us
  Pallas kernels  26.4 us (88%)
  starting transfers between devices  1.29 us (4%)
  waiting for transfers between devices  0.85 us (3%)
  between operations  0.66 us (2%)
  other arithmetic  0.6 us (2%)
    pallas_call x1, Pallas kernels, per_device(): pl.pallas_call(grads_kernel, out_shape=(jax.ShapeDtypeStruct((n8, CHP, 8...  22.6 us
    pallas_call x1, Pallas kernels, per_device(): pl.pallas_call(feature_kernel, out_shape=jax.ShapeDtypeStruct((cells, ft)...  3.74 us
    ppermute x1, starting transfers between devices, per_device(): weight_grad = wg + lax.ppermute(wg, 'lat', down)  1.29 us
    ppermute x1, waiting for transfers between devices, per_device(): weight_grad = wg + lax.ppermute(wg, 'lat', down)  0.85 us
    add x1, other arithmetic, per_device(): weight_grad = wg + lax.ppermute(wg, 'lat', down)  0.6 us
  transfers between devices with their start and end apart: 1, of which 1 were waited for; matrix products, arithmetic and copies ran while one was open for 0% of the time, Pallas kernels for 13%

profile of v5, /device:TPU:1, one launch (start us, length us, event | category | flops | bytes accessed | tf_op | source)
XLA Modules:
  0.0 29.8 jit_solution(14193675192301951380)
XLA Ops:
  0.6 22.6 %grads_and_weight_grad.1 = (bf16[8,96,1024]{2,1,0:T(8,128)(2,1)S(1)}, bf16[96,512]{1,0:T(8,128)(2,1)S(1)}, f32[16,76]{1,0:T(8,128)S(1)}) custom-call(bf16[64,128,512]{2,1,0:T(8,128)(2,1)} %feat.1, bf16[76,64,128]{2,1,0:T(8,128)(2,1)} %tgt.1, f32[6,64,128]{2,1,0:T(8,128)} %met.1, s32[4,64,128]{2,1,0:T(8,128)} %msk.1, bf16[76,512]{1,0:T(8,128)(2,1)} %bitcast.4, ...), custom_call_target="tpu_custom_call" | custom-call | flops 1610612736 | bytes 12582912 | tf_op jit(solution)/shard_map/grads_and_weight_grad/pallas_call | solution.py:563
  23.3 1.3 %collective-permute-start = (f32[16,76]{1,0:T(8,128)S(1)}, f32[16,76]{1,0:T(8,128)S(1)}, u32[]{:S(2)}, u32[]{:S(2)}) collective-permute-start(f32[16,76]{1,0:T(8,128)S(1)} %get-tuple-element.7), channel_id=1, source_target_pairs={{2,0},{3,1},{6,4},{7,5},{10,8},{11,9},{14,12},{15,13},{18,16},{19,... | collective-permute-start | bytes 14600 | tf_op jit(solution)/shard_map/ppermute | solution.py:631
  24.6 3.7 %feature_grad.1 = bf16[8192,512]{1,0:T(8,128)(2,1)} custom-call(bf16[8,96,1024]{2,1,0:T(8,128)(2,1)S(1)} %get-tuple-element.5.gr, bf16[96,512]{1,0:T(8,128)(2,1)S(1)} %get-tuple-element.6.wp), custom_call_target="tpu_custom_call" | custom-call | flops 805306368 | bytes 10485760 | tf_op jit(solution)/shard_map/feature_grad/pallas_call | solution.py:618
  28.3 0.9 %collective-permute-done = f32[16,76]{1,0:T(8,128)S(1)} collective-permute-done((f32[16,76]{1,0:T(8,128)S(1)}, f32[16,76]{1,0:T(8,128)S(1)}, u32[]{:S(2)}, u32[]{:S(2)}) %collective-permute-start) | collective-permute-done | bytes 4896 | tf_op jit(solution)/shard_map/ppermute | solution.py:631
  29.2 0.6 %add.3 = f32[16,76]{1,0:T(8,128)} add(f32[16,76]{1,0:T(8,128)S(1)} %get-tuple-element.7, f32[16,76]{1,0:T(8,128)S(1)} %collective-permute-done) | non-fusion elementwise | flops 1216 | bytes 14592 | tf_op jit(solution)/shard_map/add | solution.py:631
Async XLA Ops:
  23.3 5.9 %collective-permute-start = (f32[16,76]{1,0:T(8,128)S(1)}, f32[16,76]{1,0:T(8,128)S(1)}, u32[]{:S(2)}, u32[]{:S(2)}) collective-permute-start(f32[16,76]{1,0:T(8,128)S(1)} %get-tuple-element.7), channel_id=1, source_target_pairs={{2,0},{3,1},{6,4},{7,5},{10,8},{11,9},{14,12},{15,13},{18,16},{19,... | collective-permute-start | bytes 14600 | tf_op jit(solution)/shard_map/ppermute | solution.py:631

commit v6 on v5

--- a/solution.py
+++ b/solution.py
@@ -70,8 +70,7 @@
     ]
     for copy in small:
         copy.start()
-    @pl.loop(2, n_lon - 1)
-    def _(d):
+    for d in range(2, n_lon - 1):
         pl.semaphore_signal(
             barrier, inc=1, device_id=(lax.rem(lon + d, n_lon), lat), device_id_type=MESH
         )

time: 29.9 us -> 29.9 us (level)
  no operation moved by 1% of the time
where the time goes in v6:
time: 29.9 us; the launch traced here: 29.8 us
  Pallas kernels  26.4 us (88%)
  starting transfers between devices  1.29 us (4%)
  waiting for transfers between devices  0.85 us (3%)
  between operations  0.66 us (2%)
  other arithmetic  0.6 us (2%)
    pallas_call x1, Pallas kernels, per_device(): pl.pallas_call(grads_kernel, out_shape=(jax.ShapeDtypeStruct((n8, CHP, 8...  22.6 us
    pallas_call x1, Pallas kernels, per_device(): pl.pallas_call(feature_kernel, out_shape=jax.ShapeDtypeStruct((cells, ft)...  3.74 us
    ppermute x1, starting transfers between devices, per_device(): weight_grad = wg + lax.ppermute(wg, 'lat', down)  1.29 us
    ppermute x1, waiting for transfers between devices, per_device(): weight_grad = wg + lax.ppermute(wg, 'lat', down)  0.85 us
    add x1, other arithmetic, per_device(): weight_grad = wg + lax.ppermute(wg, 'lat', down)  0.6 us
  transfers between devices with their start and end apart: 1, of which 1 were waited for; matrix products, arithmetic and copies ran while one was open for 0% of the time, Pallas kernels for 13%

profile of v6, /device:TPU:1, one launch (start us, length us, event | category | flops | bytes accessed | tf_op | source)
XLA Modules:
  0.0 29.8 jit_solution(6471741588863744433)
XLA Ops:
  0.6 22.6 %grads_and_weight_grad.1 = (bf16[8,96,1024]{2,1,0:T(8,128)(2,1)S(1)}, bf16[96,512]{1,0:T(8,128)(2,1)S(1)}, f32[16,76]{1,0:T(8,128)S(1)}) custom-call(bf16[64,128,512]{2,1,0:T(8,128)(2,1)} %feat.1, bf16[76,64,128]{2,1,0:T(8,128)(2,1)} %tgt.1, f32[6,64,128]{2,1,0:T(8,128)} %met.1, s32[4,64,128]{2,1,0:T(8,128)} %msk.1, bf16[76,512]{1,0:T(8,128)(2,1)} %bitcast.4, ...), custom_call_target="tpu_custom_call" | custom-call | flops 1610612736 | bytes 12582912 | tf_op jit(solution)/shard_map/grads_and_weight_grad/pallas_call | solution.py:562
  23.3 1.3 %collective-permute-start = (f32[16,76]{1,0:T(8,128)S(1)}, f32[16,76]{1,0:T(8,128)S(1)}, u32[]{:S(2)}, u32[]{:S(2)}) collective-permute-start(f32[16,76]{1,0:T(8,128)S(1)} %get-tuple-element.7), channel_id=1, source_target_pairs={{2,0},{3,1},{6,4},{7,5},{10,8},{11,9},{14,12},{15,13},{18,16},{19,... | collective-permute-start | bytes 14600 | tf_op jit(solution)/shard_map/ppermute | solution.py:630
  24.6 3.7 %feature_grad.1 = bf16[8192,512]{1,0:T(8,128)(2,1)} custom-call(bf16[8,96,1024]{2,1,0:T(8,128)(2,1)S(1)} %get-tuple-element.5.gr, bf16[96,512]{1,0:T(8,128)(2,1)S(1)} %get-tuple-element.6.wp), custom_call_target="tpu_custom_call" | custom-call | flops 805306368 | bytes 10485760 | tf_op jit(solution)/shard_map/feature_grad/pallas_call | solution.py:617
  28.3 0.9 %collective-permute-done = f32[16,76]{1,0:T(8,128)S(1)} collective-permute-done((f32[16,76]{1,0:T(8,128)S(1)}, f32[16,76]{1,0:T(8,128)S(1)}, u32[]{:S(2)}, u32[]{:S(2)}) %collective-permute-start) | collective-permute-done | bytes 4896 | tf_op jit(solution)/shard_map/ppermute | solution.py:630
  29.2 0.6 %add.3 = f32[16,76]{1,0:T(8,128)} add(f32[16,76]{1,0:T(8,128)S(1)} %get-tuple-element.7, f32[16,76]{1,0:T(8,128)S(1)} %collective-permute-done) | non-fusion elementwise | flops 1216 | bytes 14592 | tf_op jit(solution)/shard_map/add | solution.py:630
Async XLA Ops:
  23.3 5.9 %collective-permute-start = (f32[16,76]{1,0:T(8,128)S(1)}, f32[16,76]{1,0:T(8,128)S(1)}, u32[]{:S(2)}, u32[]{:S(2)}) collective-permute-start(f32[16,76]{1,0:T(8,128)S(1)} %get-tuple-element.7), channel_id=1, source_target_pairs={{2,0},{3,1},{6,4},{7,5},{10,8},{11,9},{14,12},{15,13},{18,16},{19,... | collective-permute-start | bytes 14600 | tf_op jit(solution)/shard_map/ppermute | solution.py:630
